TPU v7x, 32 devices: a whole 2x2x4 slice. The times are simulated.
32 devices in a mesh: blk: 8 (over y, x, core), head: 4 (over z).
Axes of the slice: x: 2, y: 2, z: 4, core: 2. Of those that a mesh axis runs over, the one named last changes fastest.
Arguments:
- tokens: bfloat16 [4096, 2048], P(('blk', 'head')), may hold values from -6 to 6
- lengths: int32 [2], replicated, may hold values from 1024 to 2560, as said below
- block_order: int32 [32], replicated, may hold values from 0 to 31, each once
- bucket_of: int32 [257], replicated, may hold values from 0 to 31, as said below
- gain_attn: float32 [2048], P(('blk', 'head')), may hold values from 0.5 to 1.5
- w_query: bfloat16 [2048, 2048], P('blk', 'head'), may hold values from -0.015625 to 0.015625
- w_key: bfloat16 [2048, 2048], P('blk', 'head'), may hold values from -0.125 to 0.125
- w_value: bfloat16 [2048, 2048], P('blk', 'head'), may hold values from -0.125 to 0.125
- w_out: bfloat16 [2048, 2048], P('head', 'blk'), may hold values from -1.5 to 1.5
- bias_table: bfloat16 [32, 32], P('blk', 'head'), may hold values from -4 to 4
- gain_ffn: float32 [2048], P(('blk', 'head')), may hold values from 0.5 to 1.5
- w_gate: bfloat16 [2048, 5120], P('blk', 'head'), may hold values from -0.125 to 0.125
- w_up: bfloat16 [2048, 5120], P('blk', 'head'), may hold values from -0.125 to 0.125
- w_down: bfloat16 [5120, 2048], P('head', 'blk'), may hold values from -0.078125 to 0.078125
- cotangent: bfloat16 [4096, 2048], P(('blk', 'head')), may hold values from -6 to 6
Outputs:
- output: float32 [4096, 2048], P(('blk', 'head'))
- input_grad: float32 [4096, 2048], P(('blk', 'head'))
- grad_gain_attn: float32 [2048], P(('blk', 'head'))
- grad_w_query: float32 [2048, 2048], P('blk', 'head')
- grad_w_key: float32 [2048, 2048], P('blk', 'head')
- grad_w_value: float32 [2048, 2048], P('blk', 'head')
- grad_w_out: float32 [2048, 2048], P('head', 'blk')
- grad_bias_table: float32 [32, 32], P('blk', 'head')
- grad_gain_ffn: float32 [2048], P(('blk', 'head'))
- grad_w_gate: float32 [2048, 5120], P('blk', 'head')
- grad_w_up: float32 [2048, 5120], P('blk', 'head')
- grad_w_down: float32 [5120, 2048], P('head', 'blk')
Inputs may be any that keep to these rules, and one draw needn't show every extreme that they name: lengths[n] is the length of sequence n in the packed order; they add up to 4096, and one of them has exactly 2560 tokens. Rows 128 * i to 128 * i + 127 of tokens and cotangent are the places 128 * block_order[i] onward of the packed order; every block appears once. bucket_of[r + 128] is the bucket of the relative position r (key's place minus query's) for -128 <= r <= 128; farther ones take the bucket of the nearer end. For r <= 0 it lies below 16, for r > 0 at or above; for |r| < 8 it is |r|, plus 32 // 2 when r > 0; it never falls as |r| grows on either side.
All inputs are finite; a program needn't handle non-finite values.
Results may differ from a plain program's by a relative error of at most 0.024.
Values may be sent and summed in bfloat16 or wider, within the bound.
No kernel may reach another device: no remote copies, remote signals or barrier semaphores. Data moves between devices by JAX's collectives and lax.ppermute only.
A program may use at most 192 MiB of HBM per device.

v0:
```python
import functools

import jax
import jax.numpy as jnp
import numpy as np
from jax import lax
from jax.experimental import pallas as pl
from jax.experimental.pallas import tpu as pltpu
from jax.sharding import PartitionSpec as P

HD = 64
LANES = 2 * HD
MAXDIST = 128
SPAN = 128
BQ = 512
BK = BQ
NEAR = 3
WIDE = 2 * SPAN
EXTRA = 16
KT_ROWS = 80
SHIFT_ROOM = 60.0

norm_eps = 1e-06
masked_score = -1e30
f32 = jnp.float32
bf16 = jnp.bfloat16
MIB = 1 << 20
LARGE = 58 * MIB


def rms_scale(values):
    return lax.rsqrt(jnp.mean(values * values, axis=-1, keepdims=True) + norm_eps)


def norm_back(d_normed, source, inv_rms, gain_vec):
    scaled = d_normed * gain_vec
    x_hat = source * inv_rms
    gain_part = jnp.sum(d_normed * x_hat, axis=0)
    d_source = inv_rms * (scaled - x_hat * jnp.mean(scaled * x_hat, axis=-1, keepdims=True))
    return (d_source, gain_part)


def dot_nn(left, right):
    return jnp.dot(left, right, preferred_element_type=f32)


def dot_nt(left, right):
    return lax.dot_general(left, right, (((1,), (1,)), ((), ())), preferred_element_type=f32)


def dot_tn(left, right):
    return lax.dot_general(left, right, (((0,), (0,)), ((), ())), preferred_element_type=f32)


def cyclic(count, by):
    return [(i, (i + by) % count) for i in range(count)]


def together(*values):
    return lax.optimization_barrier(values)


def gather_near(rows):
    count = lax.axis_size("head")
    if count != 4:
        return [rows] + [lax.ppermute(rows, "head", cyclic(count, s)) for s in range(1, count)]
    return [rows, lax.ppermute(rows, "head", cyclic(4, 1)), lax.ppermute(rows, "head", cyclic(4, 3))]


def gather_far(near):
    if lax.axis_size("head") != 4:
        return near
    rows, back_one, ahead_one = near
    me = lax.axis_index("head")
    passed = jnp.where(me == 1, ahead_one, jnp.where(me == 2, back_one, rows))
    back_two = lax.ppermute(passed, "head", [(1, 0), (3, 1), (0, 2), (2, 3)])
    return [rows, back_one, back_two, ahead_one]


def gather_direct(rows):
    count = lax.axis_size("head")
    return [rows] + [lax.ppermute(rows, "head", cyclic(count, s)) for s in range(1, count)]


def sum_far(parts):
    count = lax.axis_size("head")
    if count != 4:
        return []
    return [lax.ppermute(parts[2], "head", [(0, 1), (1, 3), (2, 0), (3, 2)])]


def sum_near(parts, far, beside=()):
    count = lax.axis_size("head")
    if count != 4:
        return [parts[0]] + [
            lax.ppermute(parts[s], "head", cyclic(count, count - s)) for s in range(1, count)
        ], beside
    me = lax.axis_index("head")
    wide = far[0].astype(f32)
    to_back = jnp.where(me == 2, parts[1].astype(f32) + wide, parts[1].astype(f32)).astype(bf16)
    to_ahead = jnp.where(me == 1, parts[3].astype(f32) + wide, parts[3].astype(f32)).astype(bf16)
    to_back, to_ahead, *beside = together(to_back, to_ahead, *beside)
    from_ahead = lax.ppermute(to_back, "head", cyclic(4, 3))
    from_back = lax.ppermute(to_ahead, "head", cyclic(4, 1))
    return [parts[0], from_ahead, from_back, far[0]], beside


def sum_terms(terms):
    total = terms[0].astype(f32) + terms[1].astype(f32) + terms[2].astype(f32)
    if lax.axis_size("head") != 4:
        for term in terms[3:]:
            total = total + term.astype(f32)
        return total
    me = lax.axis_index("head")
    return total + jnp.where((me == 0) | (me == 3), terms[3].astype(f32), 0.0)


def is_power(count):
    return count & (count - 1) == 0


def gather_small(values):
    held = values[None]
    for axis in ("head", "blk"):
        count = lax.axis_size(axis)
        if not is_power(count):
            held = lax.all_gather(held, axis, axis=0, tiled=False)
        else:
            me = lax.axis_index(axis)
            held = held[None]
            bit = 1
            while bit < count:
                other = lax.ppermute(held, axis, [(i, i ^ bit) for i in range(count)])
                low = jnp.concatenate([held, other])
                high = jnp.concatenate([other, held])
                held = jnp.where((me // bit) % 2 == 0, low, high)
                bit *= 2
        if axis == "head":
            held = held.reshape(count, -1)
    return held


def sum_direct(parts, steps):
    count = len(parts)
    return [lax.ppermute(parts[s], "head", cyclic(count, count - s)) for s in steps]


def sum_all(terms):
    total = terms[0].astype(f32)
    for term in terms[1:]:
        total = total + term.astype(f32)
    return total


def scatter_blk(values):
    return jnp.sum(lax.all_to_all(values, "blk", 0, 0, tiled=True), axis=0)


def scatter_head(values):
    count, me = lax.axis_size("head"), lax.axis_index("head")
    total = lax.dynamic_index_in_dim(values, me, 0, False)
    for s in range(1, count):
        sent = lax.dynamic_index_in_dim(values, (me + s) % count, 0, False)
        total = total + lax.ppermute(sent, "head", cyclic(count, s))
    return total


def lane_low(shape):
    return lax.broadcasted_iota(jnp.int32, shape, 1) < HD


def swap_halves(tile):
    return pltpu.roll(tile, HD, 1)


def pair_up(first, second):
    low = lane_low(first.shape)
    return (
        jnp.where(low, first, swap_halves(second)),
        jnp.where(low, swap_halves(first), second),
    )


def project_kernel(slots, *refs):
    x_refs = refs[:slots]
    gain_ref, wq_ref, wk_ref, wv_ref, normed_ref, packed_ref, scale_ref = refs[slots:]
    rows = slots * SPAN

    @pl.when(pl.program_id(0) == 0)
    def _():
        for s in range(slots):
            wide = x_refs[s][...].astype(f32)
            scale = rms_scale(wide)
            normed = wide * scale * gain_ref[...]
            normed_ref[s * SPAN : (s + 1) * SPAN, :] = normed.astype(bf16)
            scale_ref[s * SPAN : (s + 1) * SPAN, :] = jnp.broadcast_to(scale, (SPAN, LANES))

    normed = normed_ref[...]
    query = dot_nn(normed, wq_ref[...])
    key = dot_nn(normed, wk_ref[...])
    value = dot_nn(normed, wv_ref[...])
    half = rows // 2
    for pair in range(query.shape[1] // LANES):
        cols = slice(pair * LANES, (pair + 1) * LANES)
        both = pair_up(value[:, cols], key[:, cols])
        queries = pair_up(query[:half, cols], query[half:, cols])
        for member in range(2):
            packed_ref[2 * pair + member, :rows, :] = both[member].astype(bf16)
            packed_ref[2 * pair + member, rows:, :] = queries[member].astype(bf16)


def project(x_slots, gain, weights):
    slots = len(x_slots)
    rows, depth = slots * SPAN, x_slots[0].shape[1]
    width = weights.shape[1] // 3
    heads = width // HD
    tile = min(width, 256)
    steps = width // tile
    whole = pl.BlockSpec((SPAN, depth), lambda j: (0, 0))

    def columns(part):
        return pl.BlockSpec((depth, tile), lambda j: (0, part * steps + j))

    return pl.pallas_call(
        functools.partial(project_kernel, slots),
        grid=(steps,),
        in_specs=[whole] * slots
        + [pl.BlockSpec((1, depth), lambda j: (0, 0)), columns(0), columns(1), columns(2)],
        out_specs=[
            pl.BlockSpec((rows, depth), lambda j: (0, 0)),
            pl.BlockSpec((tile // HD, rows + rows // 2, LANES), lambda j: (j, 0, 0)),
            pl.BlockSpec((rows, LANES), lambda j: (0, 0)),
        ],
        out_shape=[
            jax.ShapeDtypeStruct((rows, depth), bf16),
            jax.ShapeDtypeStruct((heads, rows + rows // 2, LANES), bf16),
            jax.ShapeDtypeStruct((rows, LANES), f32),
        ],
        compiler_params=pltpu.CompilerParams(vmem_limit_bytes=40 * MIB),
        cost_estimate=pl.CostEstimate(
            flops=10 * rows * depth * width, bytes_accessed=6 * depth * width, transcendentals=0
        ),
        name="project",
    )(*x_slots, gain, weights, weights, weights)


def place_of(order_ref, info_ref, source, slot, slots):
    z = info_ref[0]
    return order_ref[source * slots + lax.rem(z - slot + slots, slots)]


def dyn(start, size, multiple):
    return pl.ds(pl.multiple_of(start, multiple), size)


def near_blocks(bias_ref):
    tiles = []
    for c in range(NEAR):
        spread = jnp.broadcast_to(bias_ref[c : c + 1, :], (SPAN, WIDE))
        tiles.append(pltpu.roll(spread, 0, 1, stride=1, stride_axis=0)[:, :SPAN])
    return tiles


def block_step(a, b):
    return a - b + 1 if abs(a - b) <= 1 else 3 if a < b else 4


def fill_tables(bias_ref, table_ref, corner_ref):
    tiles = near_blocks(bias_ref)
    far = [jnp.broadcast_to(bias_ref[NEAR + m : NEAR + m + 1, :SPAN], (SPAN, SPAN)) for m in range(2)]
    every = tiles + far
    for a in range(BK // SPAN):
        for b in range(BQ // SPAN):
            table_ref[a * SPAN : (a + 1) * SPAN, b * SPAN : (b + 1) * SPAN] = every[block_step(a, b)]
    corner_ref[0] = tiles[0] - far[0]
    corner_ref[1] = tiles[2] - far[1]


def with_corner(tile, kind, corner):
    if kind == "prev":
        upper, lower = tile[: BK - SPAN], tile[BK - SPAN :]
        lower = jnp.concatenate([lower[:, :SPAN] + corner, lower[:, SPAN:]], axis=1)
    else:
        upper, lower = tile[:SPAN], tile[SPAN:]
        upper = jnp.concatenate([upper[:, : BQ - SPAN], upper[:, BQ - SPAN :] + corner], axis=1)
    return jnp.concatenate([upper, lower], axis=0)


def corner_of(tile, kind):
    return tile[BK - SPAN :, :SPAN] if kind == "prev" else tile[:SPAN, BQ - SPAN :]


def any_bias(bias_ref, table_ref, corner_ref, tile, block):
    left = jnp.broadcast_to(bias_ref[NEAR : NEAR + 1, 0:1], (BK, BQ))
    right = jnp.broadcast_to(bias_ref[NEAR + 1 : NEAR + 2, 0:1], (BK, BQ))
    left = with_corner(left, "prev", jnp.where(tile + 1 == block, corner_ref[0], 0.0))
    right = with_corner(right, "next", jnp.where(tile == block + 1, corner_ref[1], 0.0))
    return jnp.where(tile == block, table_ref[...], jnp.where(tile < block, left, right))


def block_range(ends_ref, q0, total):
    count = ends_ref.shape[0]
    start, end, cut = jnp.int32(0), jnp.int32(total), jnp.bool_(False)
    for n in range(count):
        edge = ends_ref[n]
        start = jnp.where(edge <= q0, edge, start)
        cut = cut | ((edge > q0) & (edge < q0 + BQ))
    for n in range(count - 1, -1, -1):
        edge = ends_ref[n]
        end = jnp.where(edge >= q0 + BQ, edge, end)
    first = lax.div(start, BK)
    last = lax.div(end + BK - 1, BK)
    whole = jnp.logical_not(cut) & (lax.rem(start, BK) == 0) & (lax.rem(end, BK) == 0)
    return first, last, whole


def row_of_tiles(first, last, block, step, left, middle, right):
    before, after = jnp.maximum(block - 1, first), jnp.minimum(block + 2, last)
    left = lax.fori_loop(first, before, functools.partial(step, "left"), left)
    left = lax.fori_loop(before, block, functools.partial(step, "prev"), left)
    middle = step("diagonal", block, left if middle is None else middle)
    right = middle if right is None else right
    right = lax.fori_loop(block + 1, after, functools.partial(step, "next"), right)
    right = lax.fori_loop(after, last, functools.partial(step, "right"), right)
    return left, middle, right


def same_sequence(ends_ref, k0, q0):
    key_place = k0 + lax.broadcasted_iota(jnp.int32, (BK, 1), 0)
    query_place = q0 + lax.broadcasted_iota(jnp.int32, (1, BQ), 1)
    key_seg = jnp.zeros((BK, 1), jnp.int32)
    query_seg = jnp.zeros((1, BQ), jnp.int32)
    for n in range(ends_ref.shape[0]):
        key_seg = key_seg + jnp.where(key_place >= ends_ref[n], 1, 0)
        query_seg = query_seg + jnp.where(query_place >= ends_ref[n], 1, 0)
    return key_seg == query_seg


def sort_blocks(order_ref, info_ref, x_ref, slots, keep):
    sources = x_ref.shape[0]
    half = slots // 2
    high = jnp.logical_not(lane_low((SPAN, LANES)))
    for source in range(sources):
        for pair in range(half):
            packed = x_ref[
                source, (slots + pair) * SPAN : (slots + pair + 1) * SPAN, :
            ].astype(f32)
            queries = (swap_halves(packed), packed)
            for member in range(2):
                slot = pair + member * half
                place = place_of(order_ref, info_ref, source, slot, slots) * SPAN
                both = x_ref[source, slot * SPAN : (slot + 1) * SPAN, :]
                keep(place, both, jnp.where(high, queries[member], 0.0).astype(bf16))


def attend_kernel(
    slots, order_ref, ends_ref, info_ref, x_ref, bias_ref, mixed_ref, exact_ref, lse_ref,
    both_ref, query_ref, turned_ref, table_ref, corner_ref, held_ref, rows_ref,
):
    total = both_ref.shape[0]
    parted = info_ref.shape[0] > 3

    def keep(place, both, query):
        both_ref[dyn(place, SPAN, SPAN), :] = both
        query_ref[dyn(place, SPAN, SPAN), :] = query
        turned = both.astype(f32).T
        turned_ref[:, dyn(place, SPAN, SPAN)] = turned[:HD, :].astype(bf16)
        turned_key, turned_query = turned[HD:, :], query.astype(f32).T[HD:, :]
        for line, product in enumerate(
            (turned_key * turned_query, turned_key * turned_key, turned_query * turned_query)
        ):
            rows_ref[line : line + 1, dyn(place, SPAN, SPAN)] = jnp.sum(
                product, axis=0, keepdims=True
            )

    sort_blocks(order_ref, info_ref, x_ref, slots, keep)
    fill_tables(bias_ref, table_ref, corner_ref)
    if parted:
        held_ref[...] = jnp.zeros_like(held_ref)
        exact_ref[...] = jnp.zeros_like(exact_ref)
        lse_ref[...] = jnp.zeros_like(lse_ref)
    left_bias = bias_ref[NEAR : NEAR + 1, 0:1]
    right_bias = bias_ref[NEAR + 1 : NEAR + 2, 0:1]
    start_state = (
        jnp.full((1, BQ), masked_score, f32),
        jnp.zeros((1, BQ), f32),
        jnp.zeros((HD, BQ), f32),
    )
    longest_key = jnp.sqrt(jnp.max(rows_ref[1:2, :], axis=1, keepdims=True))
    most_bias = jnp.max(
        jnp.max(bias_ref[: NEAR + 2, :], axis=0, keepdims=True), axis=1, keepdims=True
    )

    def one_block(block, unused):
        q0 = block * BQ
        first, last, whole = block_range(ends_ref, q0, total)
        query = query_ref[dyn(q0, BQ, BQ), :]
        own = rows_ref[0:1, dyn(q0, BQ, BQ)] + bias_ref[1:2, 0:1]
        bound = jnp.sqrt(rows_ref[2:3, dyn(q0, BQ, BQ)]) * longest_key + most_bias
        whole = whole & (jnp.max(bound - own) < SHIFT_ROOM)

        def quick_step(kind, tile, state):
            mass, mix = state
            k0 = tile * BK
            scores = dot_nt(both_ref[dyn(k0, BK, BK), :], query)
            if kind == "diagonal":
                weights = jnp.exp(scores + table_ref[...] - own)
            else:
                if kind in ("prev", "next"):
                    scores = with_corner(scores, kind, corner_ref[0 if kind == "prev" else 1])
                weights = jnp.exp(scores - (own - (left_bias if kind in ("left", "prev") else right_bias)))
            mass = mass + jnp.sum(weights, axis=0, keepdims=True)
            return (mass, mix + dot_nn(turned_ref[:, dyn(k0, BK, BK)], weights.astype(bf16)))

        def step(tile, state):
            peak, mass, mix = state
            k0 = tile * BK
            scores = dot_nt(both_ref[dyn(k0, BK, BK), :], query)
            same = same_sequence(ends_ref, k0, q0)
            scores = scores + any_bias(bias_ref, table_ref, corner_ref, tile, block)
            scores = jnp.where(same, scores, masked_score)
            new_peak = jnp.maximum(peak, jnp.max(scores, axis=0, keepdims=True))
            weights = jnp.where(same, jnp.exp(scores - new_peak), 0.0)
            rescale = jnp.exp(peak - new_peak)
            mass = mass * rescale + jnp.sum(weights, axis=0, keepdims=True)
            turned = turned_ref[:, dyn(k0, BK, BK)]
            mix = mix * rescale + dot_nn(turned, weights.astype(bf16))
            return (new_peak, mass, mix)

        def finish(peak, mass, mix):
            exact = mix / mass
            exact_ref[:, dyn(q0, BQ, BQ)] = exact
            lse_ref[:, dyn(q0, BQ, BQ)] = peak + jnp.log(mass)
            padded = jnp.concatenate([exact, exact], axis=0)
            held_ref[dyn(q0, BQ, BQ), :] = padded.T

        @pl.when(whole)
        def _():
            *unused, state = row_of_tiles(
                first, last, block, quick_step, start_state[1:], None, None
            )
            finish(own, *state)

        @pl.when(jnp.logical_not(whole))
        def _():
            finish(*lax.fori_loop(first, last, step, start_state))

        return unused

    lax.fori_loop(info_ref[1], info_ref[2], one_block, 0)
    half = slots // 2
    low = lane_low((SPAN, LANES))
    for source in range(x_ref.shape[0]):
        for pair in range(half):
            places = [
                place_of(order_ref, info_ref, source, pair + m * half, slots) * SPAN
                for m in range(2)
            ]
            tiles = [held_ref[dyn(place, SPAN, SPAN), :] for place in places]
            mixed_ref[source, pair * SPAN : (pair + 1) * SPAN, :] = jnp.where(
                low, tiles[0], tiles[1]
            ).astype(bf16)


def vmem(shape, dtype):
    return pltpu.VMEM(shape, dtype)


def smem_spec():
    return pl.BlockSpec(memory_space=pltpu.SMEM)


def vmem_spec():
    return pl.BlockSpec(memory_space=pltpu.VMEM)


def attention_vmem(total):
    return int(min(58, 16 + 44 * (total / 16384)) * MIB)


def attend(order, ends, info, swapped, bias_rows, slots):
    sources = swapped.shape[0]
    total = sources * slots * SPAN
    return pl.pallas_call(
        functools.partial(attend_kernel, slots),
        in_specs=[smem_spec()] * 3 + [vmem_spec()] * 2,
        out_specs=[vmem_spec()] * 3,
        out_shape=[
            jax.ShapeDtypeStruct((sources, slots * SPAN // 2, LANES), bf16),
            jax.ShapeDtypeStruct((HD, total), f32),
            jax.ShapeDtypeStruct((1, total), f32),
        ],
        scratch_shapes=[
            vmem((total, LANES), bf16),
            vmem((total, LANES), bf16),
            vmem((HD, total), bf16),
            vmem((BK, BQ), f32),
            vmem((2, SPAN, SPAN), f32),
            vmem((total, LANES), f32),
            vmem((8, total), f32),
        ],
        compiler_params=pltpu.CompilerParams(vmem_limit_bytes=attention_vmem(total)),
        cost_estimate=pl.CostEstimate(
            flops=total * total * 128, bytes_accessed=total * 2048, transcendentals=total * total // 2
        ),
        name="attend",
    )(order, ends, info, swapped, bias_rows)


def unroll_rows(tile):
    row = lax.broadcasted_iota(jnp.int32, tile.shape, 0)
    bit = 1
    while bit < tile.shape[0]:
        moved = pltpu.roll(tile, tile.shape[1] - bit, 1)
        tile = jnp.where((row // bit) % 2 == 1, moved, tile)
        bit *= 2
    return tile


def attend_back_kernel(
    slots, bucket_count, order_ref, ends_ref, info_ref, x_ref, mixed_ref, exact_ref, lse_ref,
    bias_ref, bucket_ref, grad_ref,
    both_ref, query_ref, back_ref, turned_ref, table_ref, corner_ref, d_block_ref, d_corner_ref,
    d_both_ref, d_query_ref, far_ref,
):
    total = both_ref.shape[0]
    sources = x_ref.shape[0]
    half = slots // 2
    low = lane_low((SPAN, LANES))

    def keep(place, both, query):
        both_ref[dyn(place, SPAN, SPAN), :] = both
        query_ref[dyn(place, SPAN, SPAN), :] = query
        turned = both.astype(f32).T
        turned_ref[:HD, dyn(place, SPAN, SPAN)] = turned[HD:, :].astype(bf16)

    sort_blocks(order_ref, info_ref, x_ref, slots, keep)
    low_half = lane_low((SPAN // 2, LANES))
    for block in range(mixed_ref.shape[0]):
        packed = mixed_ref[block].astype(f32)
        for part, tile in enumerate((packed, swap_halves(packed))):
            start = order_ref[block] * SPAN + part * (SPAN // 2)
            back_ref[dyn(start, SPAN // 2, SPAN // 2), :] = jnp.where(low_half, tile, 0.0).astype(bf16)
    fill_tables(bias_ref, table_ref, corner_ref)
    tail = lax.broadcasted_iota(jnp.int32, (KT_ROWS - HD, total), 0)
    turned_ref[HD:, :] = jnp.where(tail == 0, 1.0, 0.0).astype(bf16)
    d_block_ref[...] = jnp.zeros_like(d_block_ref)
    d_corner_ref[...] = jnp.zeros_like(d_corner_ref)
    d_both_ref[...] = jnp.zeros_like(d_both_ref)
    far_ref[...] = jnp.zeros_like(far_ref)
    if info_ref.shape[0] > 3:
        d_query_ref[...] = jnp.zeros_like(d_query_ref)
    left_bias = bias_ref[NEAR : NEAR + 1, 0:1]
    right_bias = bias_ref[NEAR + 1 : NEAR + 2, 0:1]

    def one_block(block, unused):
        q0 = block * BQ
        first, last, whole = block_range(ends_ref, q0, total)
        query = query_ref[dyn(q0, BQ, BQ), :]
        back = back_ref[dyn(q0, BQ, BQ), :]
        lse = lse_ref[:, dyn(q0, BQ, BQ)]
        turned_back = back.astype(f32).T[:HD, :]
        delta = jnp.sum(turned_back * exact_ref[:, dyn(q0, BQ, BQ)], axis=0, keepdims=True)

        def step(kind, tile, d_turned):
            k0 = tile * BK
            keys = dyn(k0, BK, BK)
            both = both_ref[keys, :]
            scores = dot_nt(both, query)
            if kind == "diagonal":
                weights = jnp.exp(scores + table_ref[...] - lse)
            elif kind == "cut":
                bias = any_bias(bias_ref, table_ref, corner_ref, tile, block)
                weights = jnp.exp(jnp.where(same_sequence(ends_ref, k0, q0), scores + bias - lse, masked_score))
            else:
                if kind in ("prev", "next"):
                    scores = with_corner(scores, kind, corner_ref[0 if kind == "prev" else 1])
                weights = jnp.exp(scores - (lse - (left_bias if kind in ("left", "prev") else right_bias)))
            d_probs = dot_nt(both, back)
            d_scores = (weights * (d_probs - delta)).astype(bf16)
            if kind == "diagonal":
                add_blocks(d_scores.astype(f32))
            elif kind in ("prev", "next"):
                m = 0 if kind == "prev" else 1
                d_corner_ref[m] = d_corner_ref[m] + corner_of(d_scores, kind).astype(f32)
            elif kind == "cut":
                wide = d_scores.astype(f32)
                sums = jnp.sum(wide, axis=0, keepdims=True)

                @pl.when(tile == block)
                def _():
                    add_blocks(wide)

                for m, (there, corner) in enumerate(
                    ((tile < block, tile + 1 == block), (tile > block, tile == block + 1))
                ):
                    far_ref[m : m + 1, :] = far_ref[m : m + 1, :] + jnp.where(there, sums, 0.0)
                    piece = corner_of(wide, ("prev", "next")[m])
                    d_corner_ref[m] = d_corner_ref[m] + jnp.where(corner, piece, 0.0)
            d_both_ref[keys, :] = (
                d_both_ref[keys, :] + dot_nn(weights.astype(bf16), back) + dot_nn(d_scores, query)
            )
            return d_turned + dot_nn(turned_ref[:, keys], d_scores)

        def add_blocks(wide):
            sums = [None] * (NEAR + 2)
            for a in range(BK // SPAN):
                for b in range(BQ // SPAN):
                    piece = wide[a * SPAN : (a + 1) * SPAN, b * SPAN : (b + 1) * SPAN]
                    at = block_step(a, b)
                    sums[at] = piece if sums[at] is None else sums[at] + piece
            for at, item in enumerate(sums):
                d_block_ref[at] = d_block_ref[at] + item

        def finish(d_turned):
            top = d_turned[:HD, :]
            d_query_ref[dyn(q0, BQ, BQ), :] = jnp.concatenate([top, top], axis=0).T.astype(bf16)

        zero = jnp.zeros((KT_ROWS, BQ), f32)

        @pl.when(whole)
        def _():
            parts = row_of_tiles(first, last, block, step, zero, zero, zero)
            for m in range(2):
                far_ref[m : m + 1, :] = far_ref[m : m + 1, :] + parts[2 * m][HD : HD + 1, :]
            finish(parts[0] + parts[1] + parts[2])

        @pl.when(jnp.logical_not(whole))
        def _():
            finish(lax.fori_loop(first, last, functools.partial(step, "cut"), zero))

        return unused

    lax.fori_loop(info_ref[1], info_ref[2], one_block, 0)

    d_blocks = [d_block_ref[0] + d_corner_ref[0], d_block_ref[1], d_block_ref[2] + d_corner_ref[1]]
    blank = jnp.zeros((SPAN, WIDE - SPAN), f32)
    sums = [
        jnp.sum(unroll_rows(jnp.concatenate([tile, blank], axis=1)), axis=0, keepdims=True)
        for tile in d_blocks
    ]
    for m in range(2):
        line = jnp.sum(d_block_ref[NEAR + m] - d_corner_ref[m], axis=0, keepdims=True)
        for b in range(BQ // SPAN):
            line = line + far_ref[m : m + 1, b * SPAN : (b + 1) * SPAN]
        sums.append(jnp.concatenate([line, blank[:1]], axis=1))
    sums = jnp.concatenate(sums, axis=0)
    buckets = bucket_ref[: NEAR + 2, :]
    by_bucket = jnp.concatenate(
        [
            jnp.sum(jnp.where(buckets == bucket, sums, 0.0), axis=0, keepdims=True)
            for bucket in range(bucket_count)
        ],
        axis=0,
    )
    totals = jnp.broadcast_to(jnp.sum(by_bucket, axis=1, keepdims=True), (bucket_count, LANES))
    upper = totals.astype(bf16).astype(f32)
    rest = totals - upper
    per_source = bucket_count // sources
    spare = jnp.zeros((EXTRA // 2 - per_source, LANES), f32)
    for source in range(sources):
        span = slice(source * per_source, (source + 1) * per_source)
        grad_ref[source, 3 * half * SPAN :, :] = jnp.concatenate(
            [upper[span], spare, rest[span], spare], axis=0
        ).astype(bf16)

    for source in range(sources):
        for pair in range(half):
            tiles = []
            for member in range(2):
                slot = pair + member * half
                place = place_of(order_ref, info_ref, source, slot, slots) * SPAN
                grad_ref[source, slot * SPAN : (slot + 1) * SPAN, :] = d_both_ref[
                    dyn(place, SPAN, SPAN), :
                ].astype(bf16)
                tiles.append(d_query_ref[dyn(place, SPAN, SPAN), :].astype(f32))
            grad_ref[source, (slots + pair) * SPAN : (slots + pair + 1) * SPAN, :] = jnp.where(
                low, tiles[0], tiles[1]
            ).astype(bf16)


def attend_back(
    order, ends, info, swapped, mixed_grad, exact, lse, bias_rows, bucket_rows, slots, bucket_count
):
    sources = swapped.shape[0]
    total = sources * slots * SPAN
    return pl.pallas_call(
        functools.partial(attend_back_kernel, slots, bucket_count),
        in_specs=[smem_spec()] * 3 + [vmem_spec()] * 6,
        out_specs=vmem_spec(),
        out_shape=jax.ShapeDtypeStruct((sources, slots * SPAN * 3 // 2 + EXTRA, LANES), bf16),
        scratch_shapes=[
            vmem((total, LANES), bf16),
            vmem((total, LANES), bf16),
            vmem((total, LANES), bf16),
            vmem((KT_ROWS, total), bf16),
            vmem((BK, BQ), f32),
            vmem((2, SPAN, SPAN), f32),
            vmem((NEAR + 2, SPAN, SPAN), f32),
            vmem((2, SPAN, SPAN), f32),
            vmem((total, LANES), f32),
            vmem((total, LANES), bf16),
            vmem((8, BQ), f32),
        ],
        compiler_params=pltpu.CompilerParams(vmem_limit_bytes=attention_vmem(total)),
        cost_estimate=pl.CostEstimate(
            flops=total * total * 320, bytes_accessed=total * 3072, transcendentals=total * total // 2
        ),
        name="attend_back",
    )(order, ends, info, swapped, mixed_grad, exact, lse, bias_rows, bucket_rows)


def out_kernel(slots, packed_ref, weight_ref, mix_ref, *part_refs):
    heads = packed_ref.shape[0]
    half = slots * SPAN // 2

    @pl.when(pl.program_id(0) == 0)
    def _():
        for pair in range(heads // 2):
            first = packed_ref[2 * pair].astype(f32)
            second = packed_ref[2 * pair + 1].astype(f32)
            top, bottom = pair_up(first, second)
            cols = slice(pair * LANES, (pair + 1) * LANES)
            mix_ref[:half, cols] = top.astype(bf16)
            mix_ref[half:, cols] = bottom.astype(bf16)

    part = dot_nn(mix_ref[...], weight_ref[...]).astype(bf16)
    for s in range(slots):
        part_refs[s][...] = part[s * SPAN : (s + 1) * SPAN]


def out_project(packed, weight, slots):
    heads = packed.shape[0]
    rows, width, depth = slots * SPAN, heads * HD, weight.shape[1]
    tile = 512
    return pl.pallas_call(
        functools.partial(out_kernel, slots),
        grid=(depth // tile,),
        in_specs=[
            pl.BlockSpec(packed.shape, lambda j: (0, 0, 0)),
            pl.BlockSpec((width, tile), lambda j: (0, j)),
        ],
        out_specs=[
            pl.BlockSpec((rows, width), lambda j: (0, 0)),
        ]
        + [pl.BlockSpec((SPAN, tile), lambda j: (0, j))] * slots,
        out_shape=[jax.ShapeDtypeStruct((rows, width), bf16)]
        + [jax.ShapeDtypeStruct((SPAN, depth), bf16)] * slots,
        compiler_params=pltpu.CompilerParams(vmem_limit_bytes=40 * MIB),
        cost_estimate=pl.CostEstimate(
            flops=2 * rows * depth * width, bytes_accessed=4 * depth * width, transcendentals=0
        ),
        name="out_project",
    )(packed, weight)


def feed_kernel(slots, *refs):
    normed_refs, grad_refs = refs[:slots], refs[slots : 2 * slots]
    gate_ref, up_ref, down_ref, active_ref, d_both_ref, rows_ref, rows_grad_ref = refs[2 * slots :]

    @pl.when(pl.program_id(0) == 0)
    def _():
        for s in range(slots):
            rows_ref[s * SPAN : (s + 1) * SPAN, :] = normed_refs[s][...]
            rows_grad_ref[s * SPAN : (s + 1) * SPAN, :] = grad_refs[s][...]

    tile = down_ref.shape[1]
    width = d_both_ref.shape[1] // 2
    gate = dot_nn(rows_ref[...], gate_ref[...])
    up = dot_nn(rows_ref[...], up_ref[...])
    d_hidden = dot_nn(rows_grad_ref[...], down_ref[...])
    scale, cubic = 0.7978845608028654, 0.044715
    square = gate * gate
    bent = jnp.tanh(scale * (gate + cubic * square * gate))
    half = 0.5 * (1.0 + bent)
    gelu = gate * half
    slope = half + 0.5 * gate * (1.0 - bent * bent) * (scale * (1.0 + 3.0 * cubic * square))
    active_ref[...] = (gelu * up).astype(bf16)
    start = pl.program_id(0) * tile
    d_both_ref[:, dyn(start, tile, tile)] = (d_hidden * up * slope).astype(bf16)
    d_both_ref[:, dyn(width + start, tile, LANES)] = (d_hidden * gelu).astype(bf16)


def feed_tile(width):
    return 256 if width % 256 == 0 else 128


def feed(normed_slots, grad_slots, weights):
    slots = len(normed_slots)
    rows, depth, width = slots * SPAN, weights.shape[0], weights.shape[1] // 3
    tile = feed_tile(width)
    steps = width // tile
    whole = pl.BlockSpec((SPAN, depth), lambda j: (0, 0))

    def columns(part):
        return pl.BlockSpec((depth, tile), lambda j: (0, part * steps + j))

    return pl.pallas_call(
        functools.partial(feed_kernel, slots),
        grid=(steps,),
        in_specs=[whole] * (2 * slots) + [columns(0), columns(1), columns(2)],
        out_specs=[
            pl.BlockSpec((rows, tile), lambda j: (0, j)),
            pl.BlockSpec((rows, 2 * width), lambda j: (0, 0)),
        ],
        out_shape=[
            jax.ShapeDtypeStruct((rows, width), bf16),
            jax.ShapeDtypeStruct((rows, 2 * width), bf16),
        ],
        scratch_shapes=[vmem((rows, depth), bf16), vmem((rows, depth), bf16)],
        compiler_params=pltpu.CompilerParams(vmem_limit_bytes=56 * MIB),
        cost_estimate=pl.CostEstimate(
            flops=6 * rows * depth * width,
            bytes_accessed=6 * depth * width,
            transcendentals=rows * width,
        ),
        name="feed",
    )(*normed_slots, *grad_slots, weights, weights, weights)


def pack_kernel(slots, shares, spot_ref, mine_ref, rest_ref, packed_ref):
    width = mine_ref.shape[1]
    half = SPAN // 2
    for s in range(slots):
        there = lax.rem(spot_ref[0] - s + slots, slots)
        for pair in range(width // LANES):
            if s == 0:
                tile = mine_ref[:, pair * LANES : (pair + 1) * LANES].astype(f32)
            else:
                start = (s - 1) * width + pair * LANES
                tile = rest_ref[:, start : start + LANES].astype(f32)
            for member, piece in enumerate(pair_up(tile[:half], tile[half:])):
                for share in range(shares):
                    packed_ref[(2 * pair + member) * shares + share, there] = piece.astype(bf16)


def pack(spot, mine, rest, shares):
    width = mine.shape[1]
    slots = 1 + rest.shape[1] // width
    return pl.pallas_call(
        functools.partial(pack_kernel, slots, shares),
        in_specs=[smem_spec(), vmem_spec(), vmem_spec()],
        out_specs=vmem_spec(),
        out_shape=jax.ShapeDtypeStruct((width // HD * shares, slots, SPAN // 2, LANES), bf16),
        compiler_params=pltpu.CompilerParams(vmem_limit_bytes=16 * MIB),
        name="pack",
    )(spot, mine, rest)


def project_back_kernel(slots, packed_ref, weight_ref, scale_ref, mix_ref, left_ref, *refs):
    x_refs, attn_refs = refs[:slots], refs[slots : 2 * slots]
    product_ref, gain_ref = refs[2 * slots : 2 * slots + 2]
    part_refs, grads_ref = refs[2 * slots + 2 : -1], refs[-1]
    heads = packed_ref.shape[0]
    rows = slots * SPAN
    half = rows // 2
    width = heads * HD

    @pl.when(pl.program_id(0) == 0)
    def _():
        for pair in range(heads // 2):
            start = pair * LANES
            tiles = [packed_ref[2 * pair + m].astype(f32) for m in range(2)]
            value, key = pair_up(tiles[0][:rows], tiles[1][:rows])
            top, bottom = pair_up(tiles[0][rows : rows + half], tiles[1][rows : rows + half])
            grads_ref[:half, start : start + LANES] = top.astype(bf16)
            grads_ref[half:, start : start + LANES] = bottom.astype(bf16)
            grads_ref[:, width + start : width + start + LANES] = key.astype(bf16)
            grads_ref[:, 2 * width + start : 2 * width + start + LANES] = value.astype(bf16)

    part = dot_nt(grads_ref[...], weight_ref[...])
    gain = jnp.zeros((1, part.shape[1]), f32)
    for s in range(slots):
        span = slice(s * SPAN, (s + 1) * SPAN)
        part_refs[s][...] = part[span].astype(bf16)
        x_hat = x_refs[s][...].astype(f32) * scale_ref[span, :1]
        gain = gain + jnp.sum(part[span] * x_hat, axis=0, keepdims=True)
    gain_ref[...] = gain
    product_ref[:, : 3 * width] = dot_tn(left_ref[...], grads_ref[...]).astype(bf16)
    attn = jnp.concatenate([ref[...] for ref in attn_refs], axis=0)
    product_ref[:, 3 * width :] = dot_tn(attn, mix_ref[...]).astype(bf16)


def project_back(packed, weights, scale, mix, left, x_slots, attn_slots):
    slots = len(x_slots)
    depth, width = weights.shape
    rows = slots * SPAN
    tile = 256
    spans = [pl.BlockSpec((SPAN, tile), lambda j: (0, j))] * slots
    total = width + mix.shape[1]
    return pl.pallas_call(
        functools.partial(project_back_kernel, slots),
        grid=(depth // tile,),
        in_specs=[
            pl.BlockSpec(packed.shape, lambda j: (0, 0, 0)),
            pl.BlockSpec((tile, width), lambda j: (j, 0)),
            pl.BlockSpec((rows, LANES), lambda j: (0, 0)),
            pl.BlockSpec(mix.shape, lambda j: (0, 0)),
            pl.BlockSpec((rows, tile), lambda j: (0, j)),
        ]
        + spans
        + spans,
        out_specs=[
            pl.BlockSpec((tile, total), lambda j: (j, 0)),
            pl.BlockSpec((1, tile), lambda j: (0, j)),
        ]
        + spans,
        out_shape=[
            jax.ShapeDtypeStruct((depth, total), bf16),
            jax.ShapeDtypeStruct((1, depth), f32),
        ]
        + [jax.ShapeDtypeStruct((SPAN, depth), bf16)] * slots,
        scratch_shapes=[vmem((rows, width), bf16)],
        compiler_params=pltpu.CompilerParams(vmem_limit_bytes=LARGE),
        cost_estimate=pl.CostEstimate(
            flops=4 * rows * depth * total, bytes_accessed=4 * depth * total, transcendentals=0
        ),
        name="project_back",
    )(packed, weights, scale, mix, left, *x_slots, *attn_slots)


def pair_kernel(slots, groups, *refs):
    left_one, left_two = refs[:slots], refs[slots : 2 * slots]
    right_one = refs[2 * slots : 2 * slots + groups]
    right_two = refs[2 * slots + groups : 2 * slots + 2 * groups]
    out_ref, right_ref = refs[-2:]
    cut = right_one[0].shape[1]

    @pl.when(pl.program_id(0) == 0)
    def _():
        start = 0
        for one, two in zip(right_one, right_two, strict=True):
            span = slice(start, start + one.shape[0])
            right_ref[span, :cut] = one[...]
            right_ref[span, cut:] = two[...]
            start += one.shape[0]

    one = jnp.concatenate([ref[...] for ref in left_one], axis=0)
    two = jnp.concatenate([ref[...] for ref in left_two], axis=0)
    out_ref[:, :cut] = dot_tn(one, right_ref[:, :cut]).astype(bf16)
    out_ref[:, cut:] = dot_tn(two, right_ref[:, cut:]).astype(bf16)


def pair_product(left_one, right_one, left_two, right_two):
    slots, groups = len(left_one), len(right_one)
    rows, depth = slots * SPAN, left_one[0].shape[1]
    width = right_one[0].shape[1] + right_two[0].shape[1]
    block = 256

    def whole(array):
        return pl.BlockSpec(array.shape, lambda j: (0, 0))

    return pl.pallas_call(
        functools.partial(pair_kernel, slots, groups),
        grid=(depth // block,),
        in_specs=[pl.BlockSpec((SPAN, block), lambda j: (0, j))] * (2 * slots)
        + [whole(piece) for piece in (*right_one, *right_two)],
        out_specs=pl.BlockSpec((block, width), lambda j: (j, 0)),
        out_shape=jax.ShapeDtypeStruct((depth, width), bf16),
        scratch_shapes=[vmem((rows, width), bf16)],
        compiler_params=pltpu.CompilerParams(vmem_limit_bytes=32 * MIB),
        cost_estimate=pl.CostEstimate(
            flops=2 * rows * depth * width, bytes_accessed=2 * depth * width, transcendentals=0
        ),
        name="pair_product",
    )(*left_one, *left_two, *right_one, *right_two)


def bucket_lines(bucket_of):
    count = bucket_of.shape[0]
    turned = bucket_of[::-1]
    ends = [jnp.broadcast_to(end, (2 * SPAN,)) for end in (turned[:1], turned[-1:])]
    padded = jnp.concatenate([ends[0], turned, ends[1]])
    zero_at = 2 * SPAN + count // 2
    rows = []
    for c in range(NEAR):
        base = zero_at - (c - 1) * SPAN
        rows.append(jnp.concatenate([padded[base : base + SPAN], padded[base - SPAN : base]]))
    rows.append(jnp.broadcast_to(bucket_of[:1], (WIDE,)))
    rows.append(jnp.broadcast_to(bucket_of[-1:], (WIDE,)))
    spare = 8 - (NEAR + 2)
    return jnp.concatenate([jnp.stack(rows), jnp.full((spare, WIDE), -1, bucket_of.dtype)])


def on_device(
    tokens,
    lengths,
    block_order,
    bucket_of,
    gain_attn,
    w_query,
    w_key,
    w_value,
    w_out,
    bias_table,
    gain_ffn,
    w_gate,
    w_up,
    w_down,
    cotangent,
):
    blk_count, slots = lax.axis_size("blk"), lax.axis_size("head")
    blk_spot, head_spot = lax.axis_index("blk"), lax.axis_index("head")
    depth = tokens.shape[1]
    width = w_query.shape[1]
    heads = width // HD
    shares = blk_count // heads
    table_rows, table_heads = bias_table.shape
    bucket_count = table_rows * blk_count
    total = blk_count * slots * SPAN
    gain_size = gain_attn.shape[0]
    hidden = w_gate.shape[1]

    token_slots = gather_far(gather_near(tokens))
    small = gather_small(
        jnp.concatenate([gain_attn, gain_ffn, bias_table.astype(f32).reshape(-1)])
    )
    full_qkv = lax.all_gather(
        jnp.concatenate([w_query, w_key, w_value], axis=1), "blk", axis=0, tiled=True
    )
    full_out = lax.all_gather(w_out, "blk", axis=1, tiled=True)
    full_ffn = lax.all_gather(
        jnp.concatenate([w_gate, w_up, w_down.T], axis=1), "blk", axis=0, tiled=True
    )
    gain_one = small[:, :, :gain_size].reshape(1, depth)
    gain_two = small[:, :, gain_size : 2 * gain_size].reshape(1, depth)

    tables = lax.dynamic_index_in_dim(small, head_spot, 1, False)[:, 2 * gain_size :]
    tables = tables.reshape(bucket_count, table_heads)
    my_head = blk_spot // shares
    my_bias = lax.dynamic_index_in_dim(tables, my_head, 1, False)
    bucket_rows = bucket_lines(bucket_of)
    bias_rows = jnp.sum(
        jnp.where(
            bucket_rows[None] == jnp.arange(bucket_count, dtype=jnp.int32)[:, None, None],
            my_bias[:, None, None],
            0.0,
        ),
        axis=0,
    )
    ends = jnp.cumsum(lengths).astype(jnp.int32)
    per_share = total // BQ // shares
    start = (blk_spot % shares) * per_share
    info = [head_spot, start, start + per_share] + ([start] if shares > 1 else [])
    info = jnp.stack([jnp.asarray(item, jnp.int32) for item in info])

    def swap(values):
        return lax.all_to_all(values, "blk", 0, 0, tiled=True)

    def to_all(values):
        values = values.reshape((blk_count * slots,) + values.shape[2:])
        return lax.all_to_all(values, ("blk", "head"), 0, 0, tiled=True)

    def to_heads(values):
        return swap(values if shares == 1 else jnp.repeat(values, shares, axis=0))

    def to_rows(values):
        values = swap(values)
        if shares == 1:
            return values
        values = values.reshape((heads, shares) + values.shape[1:])
        return jnp.sum(values.astype(f32), axis=1).astype(bf16)

    w_out, cotangent, *token_slots = together(w_out, cotangent, *token_slots)
    normed_one, packed, scale_one = project(token_slots, gain_one, full_qkv)
    early = (ends, info, bias_rows, bucket_rows)
    swapped, ends, info, bias_rows, bucket_rows, *out_near = together(
        to_heads(packed), *early, *gather_near(w_out)
    )
    grad_near, out_slots = gather_near(cotangent), gather_far(out_near)
    mixed, exact, lse = attend(block_order, ends, info, swapped, bias_rows, slots)
    mixed, *moved = together(mixed, *grad_near, *out_slots)
    grad_near, out_slots = moved[: len(grad_near)], moved[len(grad_near) :]
    packed_mix, *grad_slots = together(to_rows(mixed), *gather_far(grad_near))
    attn_mix, *out_parts = out_project(packed_mix, full_out, slots)
    out_parts, out_slots = together(out_parts, out_slots)
    full_rest = lax.all_gather(jnp.concatenate(out_slots[1:]), "blk", axis=1, tiled=True)
    tokens_wide = tokens.astype(f32)
    hidden_one = tokens_wide + sum_terms(sum_near(out_parts, sum_far(out_parts))[0])
    rstd_two = rms_scale(hidden_one)
    normed_two = (hidden_one * rstd_two * gain_two).astype(bf16)

    normed_slots = gather_far(gather_near(normed_two))
    active, d_both = feed(normed_slots, grad_slots, full_ffn)

    def spans(rows):
        return [rows[s * SPAN : (s + 1) * SPAN] for s in range(rows.shape[0] // SPAN)]

    d_parts = spans(dot_nt(d_both, full_ffn[:, : 2 * hidden]).astype(bf16))
    d_far = sum_far(d_parts)
    grad_hidden, *d_far = together(
        pair_product(normed_slots, [d_both], grad_slots, [active]), *d_far
    )
    grad_hidden = lax.psum_scatter(grad_hidden, "blk", scatter_dimension=0, tiled=True)
    d_near, (active,) = sum_near(d_parts, d_far, (active,))
    down_rows = dot_nt(active, full_ffn[:, 2 * hidden :]).astype(bf16)
    down_rows, full_rest, *d_near = together(down_rows, full_rest, *d_near)
    down_parts = spans(down_rows)
    d_normed_two = sum_terms(d_near)
    d_source_two, gain_part_two = norm_back(d_normed_two, hidden_one, rstd_two, gain_two)
    d_hidden_one = cotangent.astype(f32) + d_source_two

    d_attn = d_hidden_one.astype(bf16)
    mix_grads = pack(
        jnp.reshape(head_spot, (1,)).astype(jnp.int32),
        dot_nt(d_attn, full_out).astype(bf16),
        dot_nt(d_attn, full_rest).astype(bf16),
        shares,
    )
    mix_grads, d_attn = together(mix_grads, d_attn)
    middle = slots // 2
    steps = [t for t in range(1, slots) if t != middle]
    moved = (*gather_near(d_attn), *sum_direct(down_parts, steps))
    grads = attend_back(
        block_order, ends, info, swapped, to_all(mix_grads), exact, lse, bias_rows, bucket_rows,
        slots, bucket_count,
    )
    grads, *moved = together(grads, *moved)
    attn_near, down_terms = moved[: 2 - slots], moved[2 - slots :]
    grads, *attn_slots = together(swap(grads), *gather_far(attn_near))
    extra = grads[:, -EXTRA:, 0].astype(f32).reshape(blk_count, 2, -1).sum(axis=1)
    grad_table = extra[:, :table_rows].reshape(heads, shares, table_rows).sum(axis=1).T
    if shares > 1:
        grads = grads.reshape((heads, shares) + grads.shape[1:])
        grads = jnp.sum(grads.astype(f32), axis=1).astype(bf16)
    grad_heads, gain_part_one, *one_parts = project_back(
        grads, full_qkv, scale_one, attn_mix, normed_one, token_slots, attn_slots
    )

    one_far = sum_far(one_parts)
    gain_parts = jnp.stack(
        [part.reshape(blk_count, slots, gain_size) for part in (gain_part_one, gain_part_two)],
        axis=2,
    )
    grad_heads, grad_hidden = together(grad_heads, grad_hidden)
    gain_parts, *one_far = together(gain_parts, *one_far)
    grad_heads = lax.psum_scatter(grad_heads, "blk", scatter_dimension=0, tiled=True).astype(f32)
    one_near, unused = sum_near(one_parts, one_far)
    gain_sums = scatter_blk(gain_parts)
    gain_sums, down_parts, grad_hidden, *one_near = together(
        gain_sums, down_parts, grad_hidden, *one_near
    )
    gain_sums = scatter_head(gain_sums)
    grad_hidden = grad_hidden.astype(f32)
    output = hidden_one + sum_all([down_parts[0]] + down_terms + sum_direct(down_parts, [middle]))
    d_normed_one = sum_terms(one_near)
    d_source_one, unused = norm_back(d_normed_one, tokens_wide, rms_scale(tokens_wide), gain_one)
    input_grad = d_hidden_one + d_source_one
    return (
        output,
        input_grad,
        gain_sums[0],
        grad_heads[:, :width],
        grad_heads[:, width : 2 * width],
        grad_heads[:, 2 * width : 3 * width],
        grad_heads[:, 3 * width :].T,
        grad_table,
        gain_sums[1],
        grad_hidden[:, :hidden],
        grad_hidden[:, hidden : 2 * hidden],
        grad_hidden[:, 2 * hidden :].T,
    )


def solution(mesh):
    rows, spread = P(("blk", "head"), None), P(("blk", "head"))
    inward, outward = P("blk", "head"), P("head", "blk")
    in_specs = (
        rows, P(), P(), P(), spread, inward, inward, inward, outward, inward, spread,
        inward, inward, outward, rows,
    )
    out_specs = (
        rows, rows, spread, inward, inward, inward, outward, inward, spread,
        inward, inward, outward,
    )
    return jax.shard_map(
        on_device, mesh=mesh, in_specs=in_specs, out_specs=out_specs, check_vma=False
    )
```

profile of v0, /device:TPU:0, one launch (start us, length us, event | category | flops | bytes accessed | tf_op | source)
XLA Modules:
  0.0 497.0 jit_solution(16224124244922882604)
XLA Ops:
  17.4 22.3 %collective-permute-done.3 = f32[1,1,160]{2,0,1:T(1,128)S(1)} collective-permute-done((f32[1,1,160]{2,0,1:T(1,128)S(1)}, f32[1,1,160]{2,0,1:T(1,128)S(1)}, u32[]{:S(2)}, u32[]{:S(2)}) %collective-permute-start.3) | collective-permute-done | bytes 672 | tf_op jit(solution)/shard_map/ppermute | solution.py:133
  93.7 7.6 %all-to-all-done.x_ref = bf16[8,768,128]{2,1,0:T(8,128)(2,1)} async-done(((bf16[8,768,128]{2,1,0:T(8,128)(2,1)}), bf16[8,768,128]{2,1,0:T(8,128)(2,1)}, u32[]{:S(2)}, u32[]{:S(2)}) %all-to-all-start) | async-done | bytes 1572896 | tf_op jit(solution)/shard_map/all_to_all | solution.py:1048
  103.8 22.0 %attend.1 = (bf16[8,256,128]{2,1,0:T(8,128)(2,1)S(1)}, f32[64,4096]{1,0:T(8,128)S(1)}, f32[1,4096]{1,0:T(1,128)S(1)}) custom-call(s32[32]{0:T(128)S(1)} %copy-done.35, s32[2]{0:T(128)S(1)} %bitcast.44, s32[3]{0:T(128)S(1)} %pad_add_fusion.2.info_ref, bf16[8,768,128]{2,1,0:T(8,128)(2,1)} %all-to-all-done.x_ref, f32[8,256]{1,0:T(8,128)S(1)} %select_reduce_fusion.bias_ref), custom_call_target="tpu_custom_call" | custom-call | flops 2147483648 | bytes 8388608 | tf_op jit(solution)/shard_map/attend/pallas_call | solution.py:484
  127.6 13.2 %all_to_all.25.packed_ref = bf16[8,256,128]{2,1,0:T(8,128)(2,1)} all-to-all(bf16[8,256,128]{2,1,0:T(8,128)(2,1)S(1)} %get-tuple-element.119), channel_id=1, replica_groups=mesh['blk'=8,'head'=4] {'blk'}, dimensions={0} | all-to-all | bytes 1048576 | tf_op jit(solution)/shard_map/all_to_all | solution.py:1048
  151.2 12.0 %collective-permute-done.14 = bf16[128,2048]{1,0:T(8,128)(2,1)S(1)} collective-permute-done((bf16[128,2048]{1,0:T(8,128)(2,1)S(1)}, bf16[128,2048]{1,0:T(8,128)(2,1)S(1)}, u32[]{:S(2)}, u32[]{:S(2)}) %collective-permute-start.14) | collective-permute-done | bytes 524320 | tf_op jit(solution)/shard_map/ppermute | solution.py:89
  168.3 13.0 %collective-permute-done.16 = bf16[128,2048]{1,0:T(8,128)(2,1)S(1)} collective-permute-done((bf16[128,2048]{1,0:T(8,128)(2,1)}, bf16[128,2048]{1,0:T(8,128)(2,1)S(1)}, u32[]{:S(2)}, u32[]{:S(2)}) %collective-permute-start.16) | collective-permute-done | bytes 524320 | tf_op jit(solution)/shard_map/ppermute | solution.py:104
  181.2 6.5 %collective-permute-done.15 = bf16[128,2048]{1,0:T(8,128)(2,1)S(1)} collective-permute-done((bf16[128,2048]{1,0:T(8,128)(2,1)S(1)}, bf16[128,2048]{1,0:T(8,128)(2,1)S(1)}, u32[]{:S(2)}, u32[]{:S(2)}) %collective-permute-start.15) | collective-permute-done | bytes 524320 | tf_op jit(solution)/shard_map/ppermute | solution.py:103
  192.5 12.7 %collective-permute-done.17.refs_1_ = bf16[128,2048]{1,0:T(8,128)(2,1)S(1)} collective-permute-done((bf16[128,2048]{1,0:T(8,128)(2,1)S(1)}, bf16[128,2048]{1,0:T(8,128)(2,1)S(1)}, u32[]{:S(2)}, u32[]{:S(2)}) %collective-permute-start.17) | collective-permute-done | bytes 524320 | tf_op jit(solution)/shard_map/ppermute | solution.py:67
  205.2 8.5 %collective-permute-done.18.refs_3_ = bf16[128,2048]{1,0:T(8,128)(2,1)S(1)} collective-permute-done((bf16[128,2048]{1,0:T(8,128)(2,1)S(1)}, bf16[128,2048]{1,0:T(8,128)(2,1)S(1)}, u32[]{:S(2)}, u32[]{:S(2)}) %collective-permute-start.18) | collective-permute-done | bytes 524320 | tf_op jit(solution)/shard_map/ppermute | solution.py:67
  214.7 13.3 %collective-permute-done.19.refs_2_ = bf16[128,2048]{1,0:T(8,128)(2,1)S(1)} collective-permute-done((bf16[128,2048]{1,0:T(8,128)(2,1)S(1)}, bf16[128,2048]{1,0:T(8,128)(2,1)S(1)}, u32[]{:S(2)}, u32[]{:S(2)}) %collective-permute-start.19) | collective-permute-done | bytes 524320 | tf_op jit(solution)/shard_map/ppermute | solution.py:76
  228.8 15.2 %feed.1 = (bf16[512,1280]{1,0:T(8,128)(2,1)}, bf16[512,2560]{1,0:T(8,128)(2,1)}) custom-call(bf16[128,2048]{1,0:T(8,128)(2,1)} %copy-done.5, bf16[128,2048]{1,0:T(8,128)(2,1)} %copy-done.11, bf16[128,2048]{1,0:T(8,128)(2,1)} %copy-done.22, bf16[128,2048]{1,0:T(8,128)(2,1)} %copy-done.13, bf16[128,2048]{1,0:T(8,128)(2,1)} %refs_4_.1, ...), custom_call_target="tpu_custom_call" | custom-call | flops 8053063680 | bytes 15728640 | tf_op jit(solution)/shard_map/feed/pallas_call | solution.py:798
  244.1 9.3 %fusion.4 = bf16[512,2048]{1,0:T(8,128)(2,1)S(1)} fusion(bf16[512,2560]{1,0:T(8,128)(2,1)} %get-tuple-element.141.refs_8_, bf16[2048,3840]{1,0:T(8,128)(2,1)} %all-gather.9.cloned.1.call-done.refs_8_.refs_9_.refs_10_), kind=kOutput, calls=%fused_computation.4 | convolution fusion | flops 5369757696 | bytes 15204352 | tf_op jit(solution)/shard_map/dot_general | solution.py:48
  256.2 12.4 %pair_product.1 = bf16[2048,3840]{1,0:T(8,128)(2,1)} custom-call(bf16[128,2048]{1,0:T(8,128)(2,1)S(1)} %copy-done.6, bf16[128,2048]{1,0:T(8,128)(2,1)S(1)} %copy-done.12, bf16[128,2048]{1,0:T(8,128)(2,1)S(1)} %copy-done.23, bf16[128,2048]{1,0:T(8,128)(2,1)S(1)} %copy-done.14, bf16[128,2048]{1,0:T(8,128)(2,1)S(1)} %copy-done.4, ...), custom_call_target="tpu_custom_call" | custom-call | flops 8053063680 | bytes 15728640 | tf_op jit(solution)/shard_map/pair_product/pallas_call | solution.py:953
  273.3 7.8 %fusion.7 = bf16[512,2048]{1,0:T(8,128)(2,1)} fusion(bf16[512,1280]{1,0:T(8,128)(2,1)S(1)} %copy-done.31, bf16[2048,3840]{1,0:T(8,128)(2,1)} %all-gather.9.cloned.1.call-done.refs_8_.refs_9_.refs_10_), kind=kOutput, calls=%fused_computation.5 | convolution fusion | flops 2685403136 | bytes 8650752 | tf_op jit(solution)/shard_map/dot_general | solution.py:48
  285.2 11.0 %collective-permute-done.22 = bf16[128,2048]{1,0:T(8,128)(2,1)} collective-permute-done((bf16[128,2048]{1,0:T(8,128)(2,1)}, bf16[128,2048]{1,0:T(8,128)(2,1)}, u32[]{:S(2)}, u32[]{:S(2)}) %collective-permute-start.22) | collective-permute-done | bytes 524320 | tf_op jit(solution)/shard_map/ppermute | solution.py:104
  300.7 6.0 %convolution_convert_fusion.rest_ref = bf16[128,1536]{1,0:T(8,128)(2,1)S(1)} fusion(bf16[128,2048]{1,0:T(8,128)(2,1)S(1)} %fusion.25.refs_4_, bf16[1536,2048]{1,0:T(8,128)(2,1)} %all-gather.11.cloned.1.call-done), kind=kOutput, calls=%fused_computation.6 | convolution fusion | flops 805502976 | bytes 7208960 | tf_op jit(solution)/shard_map/dot_general | solution.py:48
  322.0 16.3 %all-to-all-done.2.mixed_ref = bf16[32,64,128]{2,1,0:T(8,128)(2,1)S(1)} async-done(((bf16[32,64,128]{2,1,0:T(8,128)(2,1)}), bf16[32,64,128]{2,1,0:T(8,128)(2,1)S(1)}, u32[]{:S(2)}, u32[]{:S(2)}) %all-to-all-start.2) | async-done | bytes 524320 | tf_op jit(solution)/shard_map/all_to_all | solution.py:1052
  338.4 35.3 %attend_back.1 = bf16[8,784,128]{2,1,0:T(8,128)(2,1)} custom-call(s32[32]{0:T(128)S(1)} %copy-done.35, s32[2]{0:T(128)S(1)} %bitcast.45, s32[3]{0:T(128)S(1)} %pad_add_fusion.2.info_ref, bf16[8,768,128]{2,1,0:T(8,128)(2,1)} %all-to-all-done.x_ref, bf16[32,64,128]{2,1,0:T(8,128)(2,1)S(1)} %all-to-all-done.2.mixed_ref, f32[64,4096]{1,0:T(8,128)S(1)} %copy-done.38, ...), custom_call_target="tpu_custom_call" | custom-call | flops 5368709120 | bytes 12582912 | tf_op jit(solution)/shard_map/attend_back/pallas_call | solution.py:687
  380.3 14.2 %collective-permute-done.27.refs_6_ = bf16[128,2048]{1,0:T(8,128)(2,1)S(1)} collective-permute-done((bf16[128,2048]{1,0:T(8,128)(2,1)S(1)}, bf16[128,2048]{1,0:T(8,128)(2,1)S(1)}, u32[]{:S(2)}, u32[]{:S(2)}) %collective-permute-start.27) | collective-permute-done | bytes 524320 | tf_op jit(solution)/shard_map/ppermute | solution.py:76
  399.8 15.3 %project_back.1 = (bf16[2048,2048]{1,0:T(8,128)(2,1)}, f32[1,2048]{1,0:T(1,128)}, bf16[128,2048]{1,0:T(8,128)(2,1)}, bf16[128,2048]{1,0:T(8,128)(2,1)}, bf16[128...) custom-call(bf16[8,784,128]{2,1,0:T(8,128)(2,1)} %all-to-all-done.3.packed_ref, ...), custom_call_target="tpu_custom_call" | custom-call | flops 8589934592 | bytes 16777216 | tf_op jit(solution)/shard_map/project_back/pallas_call | solution.py:891
  419.1 8.2 %collective-permute-done.28 = bf16[128,2048]{1,0:T(8,128)(2,1)S(1)} collective-permute-done((bf16[128,2048]{1,0:T(8,128)(2,1)}, bf16[128,2048]{1,0:T(8,128)(2,1)S(1)}, u32[]{:S(2)}, u32[]{:S(2)}) %collective-permute-start.28) | collective-permute-done | bytes 524320 | tf_op jit(solution)/shard_map/ppermute | solution.py:89
  444.7 7.2 %collective-permute-done.30 = bf16[128,2048]{1,0:T(8,128)(2,1)S(1)} collective-permute-done((bf16[128,2048]{1,0:T(8,128)(2,1)}, bf16[128,2048]{1,0:T(8,128)(2,1)S(1)}, u32[]{:S(2)}, u32[]{:S(2)}) %collective-permute-start.30) | collective-permute-done | bytes 524320 | tf_op jit(solution)/shard_map/ppermute | solution.py:104
  465.7 8.8 %collective-permute-done.33 = f32[2,64]{1,0:T(2,128)S(1)} collective-permute-done((f32[2,64]{1,0:T(2,128)S(1)}, f32[2,64]{1,0:T(2,128)S(1)}, u32[]{:S(2)}, u32[]{:S(2)}) %collective-permute-start.33) | collective-permute-done | bytes 544 | tf_op jit(solution)/shard_map/ppermute | solution.py:164
  479.8 6.1 %reduce-scatter.5.cloned.1.call-done = bf16[256,2048]{1,0:T(8,128)(2,1)} async-done(((bf16[2048,2048]{1,0:T(8,128)(2,1)}), bf16[256,2048]{1,0:T(8,128)(2,1)}) %reduce-scatter.5.cloned.1.call-update) | async-done | bytes 1048592 | tf_op jit(solution)/shard_map/reduce_scatter | solution.py:1137
  (311 shorter events, 177.2 us)
Async XLA Ops:
  7.2 51.9 %all-gather.5.cloned.1.call-start = ((), (), s32[]{:S(2)}) async-start(), calls=%async_computation.7 | async-start | bytes 7077888 | tf_op jit(solution)/shard_map/all_gather | solution.py:1018
  9.4 131.4 %all-gather.7.cloned.1.call-start = ((), (), s32[]{:S(2)}) async-start(), calls=%async_computation.8 | async-start | bytes 2359296 | tf_op jit(solution)/shard_map/all_gather | solution.py:1021
  10.2 217.8 %all-gather.9.cloned.1.call-start = ((), (), s32[]{:S(2)}) async-start(), calls=%async_computation.9 | async-start | bytes 17694720 | tf_op jit(solution)/shard_map/all_gather | solution.py:1022
  12.0 32.4 %collective-permute-start = (bf16[128,2048]{1,0:T(8,128)(2,1)S(1)}, bf16[128,2048]{1,0:T(8,128)(2,1)S(1)}, u32[]{:S(2)}, u32[]{:S(2)}) collective-permute-start(bf16[128,2048]{1,0:T(8,128)(2,1)S(1)} %copy-done.1), channel_id=1, source_target_pairs={{0,1},{1,2},{2,3},{3,0},{4,5},{5,6},{6,7},{7,4},{8,9},{9,10},{10,1... | collective-permute-start | bytes 1572872 | tf_op jit(solution)/shard_map/ppermute | solution.py:67
  15.1 29.4 %collective-permute-start.1 = (bf16[128,2048]{1,0:T(8,128)(2,1)S(1)}, bf16[128,2048]{1,0:T(8,128)(2,1)S(1)}, u32[]{:S(2)}, u32[]{:S(2)}) collective-permute-start(bf16[128,2048]{1,0:T(8,128)(2,1)S(1)} %copy-done.1), channel_id=1, source_target_pairs={{0,3},{1,0},{2,1},{3,2},{4,7},{5,4},{6,5},{7,6},{8,11},{9,8},{10,9... | collective-permute-start | bytes 1572872 | tf_op jit(solution)/shard_map/ppermute | solution.py:67
  17.3 22.4 %collective-permute-start.3 = (f32[1,1,160]{2,0,1:T(1,128)S(1)}, f32[1,1,160]{2,0,1:T(1,128)S(1)}, u32[]{:S(2)}, u32[]{:S(2)}) collective-permute-start(f32[1,1,160]{2,0,1:T(1,128)S(1)} %bitcast.50), channel_id=1, source_target_pairs={{0,1},{1,0},{2,3},{3,2},{4,5},{5,4},{6,7},{7,6},{8,9},{9,8},{10,11... | collective-permute-start | bytes 1928 | tf_op jit(solution)/shard_map/ppermute | solution.py:133
  70.2 31.1 %all-to-all-start = ((bf16[8,768,128]{2,1,0:T(8,128)(2,1)}), bf16[8,768,128]{2,1,0:T(8,128)(2,1)}, u32[]{:S(2)}, u32[]{:S(2)}) async-start(bf16[8,768,128]{2,1,0:T(8,128)(2,1)} %copy-done.19), calls=%async_computation | async-start | bytes 3145728 | tf_op jit(solution)/shard_map/all_to_all | solution.py:1048
  74.6 206.4 %all-gather.11.cloned.1.call-start = ((), (), s32[]{:S(2)}) async-start(), calls=%async_computation.10 | async-start | bytes 7077888 | tf_op jit(solution)/shard_map/all_gather | solution.py:1077
  82.8 43.1 %collective-permute-start.10 = (bf16[128,2048]{1,0:T(8,128)(2,1)S(1)}, bf16[128,2048]{1,0:T(8,128)(2,1)S(1)}, u32[]{:S(2)}, u32[]{:S(2)}) collective-permute-start(bf16[128,2048]{1,0:T(8,128)(2,1)S(1)} %copy-done.3), channel_id=1, source_target_pairs={{0,1},{1,2},{2,3},{3,0},{4,5},{5,6},{6,7},{7,4},{8,9},{9,10},{10,1... | collective-permute-start | bytes 1572872 | tf_op jit(solution)/shard_map/ppermute | solution.py:67
  82.8 43.0 %collective-permute-start.11 = (bf16[128,2048]{1,0:T(8,128)(2,1)S(1)}, bf16[128,2048]{1,0:T(8,128)(2,1)S(1)}, u32[]{:S(2)}, u32[]{:S(2)}) collective-permute-start(bf16[128,2048]{1,0:T(8,128)(2,1)S(1)} %copy-done.3), channel_id=1, source_target_pairs={{0,3},{1,0},{2,1},{3,2},{4,7},{5,4},{6,5},{7,6},{8,11},{9,8},{10,9... | collective-permute-start | bytes 1572872 | tf_op jit(solution)/shard_map/ppermute | solution.py:67
  101.3 24.6 %collective-permute-start.12 = (bf16[512,256]{1,0:T(8,128)(2,1)S(1)}, bf16[512,256]{1,0:T(8,128)(2,1)S(1)}, u32[]{:S(2)}, u32[]{:S(2)}) collective-permute-start(bf16[512,256]{1,0:T(8,128)(2,1)S(1)} %select_select_fusion.4), channel_id=1, source_target_pairs={{1,0},{3,1},{0,2},{2,3},{5,4},{7,5},{4,6},{6,7},{9,8},{11,9},{8,10... | collective-permute-start | bytes 786440 | tf_op jit(solution)/shard_map/ppermute | solution.py:76
  149.4 265.7 %reduce-scatter.3.cloned.1.call-start = ((), (), s32[]{:S(2)}) async-start(), calls=%async_computation.11 | async-start | bytes 17694720 | tf_op jit(solution)/shard_map/reduce_scatter | solution.py:1094
  164.9 22.7 %collective-permute-start.15 = (bf16[128,2048]{1,0:T(8,128)(2,1)S(1)}, bf16[128,2048]{1,0:T(8,128)(2,1)S(1)}, u32[]{:S(2)}, u32[]{:S(2)}) collective-permute-start(bf16[128,2048]{1,0:T(8,128)(2,1)S(1)} %get-tuple-element.135), channel_id=1, source_target_pairs={{0,3},{1,0},{2,1},{3,2},{4,7},{5,4},{6,5},{7,6},{8,11},{9,8},{10,9... | collective-permute-start | bytes 1572872 | tf_op jit(solution)/shard_map/ppermute | solution.py:103
  190.2 23.5 %collective-permute-start.18 = (bf16[128,2048]{1,0:T(8,128)(2,1)S(1)}, bf16[128,2048]{1,0:T(8,128)(2,1)S(1)}, u32[]{:S(2)}, u32[]{:S(2)}) collective-permute-start(bf16[128,2048]{1,0:T(8,128)(2,1)S(1)} %multiply_convert_fusion.refs_0_), channel_id=1, source_target_pairs={{0,3},{1,0},{2,1},{3,2},{4,7},{5,4},{6,5},{7,6},{8,11},{9,8},{10,9... | collective-permute-start | bytes 1572872 | tf_op jit(solution)/shard_map/ppermute | solution.py:67
  272.1 24.1 %collective-permute-start.22 = (bf16[128,2048]{1,0:T(8,128)(2,1)}, bf16[128,2048]{1,0:T(8,128)(2,1)}, u32[]{:S(2)}, u32[]{:S(2)}) collective-permute-start(bf16[128,2048]{1,0:T(8,128)(2,1)} %get-tuple-element.149), channel_id=1, source_target_pairs={{0,1},{1,2},{2,3},{3,0},{4,5},{5,6},{6,7},{7,4},{8,9},{9,10},{10,1... | collective-permute-start | bytes 1572872 | tf_op jit(solution)/shard_map/ppermute | solution.py:104
  307.7 30.7 %all-to-all-start.2 = ((bf16[32,64,128]{2,1,0:T(8,128)(2,1)}), bf16[32,64,128]{2,1,0:T(8,128)(2,1)S(1)}, u32[]{:S(2)}, u32[]{:S(2)}) async-start(bf16[32,64,128]{2,1,0:T(8,128)(2,1)} %bitcast.14), calls=%async_computation.2 | async-start | bytes 1048576 | tf_op jit(solution)/shard_map/all_to_all | solution.py:1052
  312.9 60.8 %collective-permute-start.23 = (bf16[128,2048]{1,0:T(8,128)(2,1)}, bf16[128,2048]{1,0:T(8,128)(2,1)}, u32[]{:S(2)}, u32[]{:S(2)}) collective-permute-start(bf16[128,2048]{1,0:T(8,128)(2,1)} %copy-done.44), channel_id=1, source_target_pairs={{0,1},{1,2},{2,3},{3,0},{4,5},{5,6},{6,7},{7,4},{8,9},{9,10},{10,1... | collective-permute-start | bytes 1572872 | tf_op jit(solution)/shard_map/ppermute | solution.py:67
  314.7 59.0 %collective-permute-start.24 = (bf16[128,2048]{1,0:T(8,128)(2,1)}, bf16[128,2048]{1,0:T(8,128)(2,1)}, u32[]{:S(2)}, u32[]{:S(2)}) collective-permute-start(bf16[128,2048]{1,0:T(8,128)(2,1)} %copy-done.44), channel_id=1, source_target_pairs={{0,3},{1,0},{2,1},{3,2},{4,7},{5,4},{6,5},{7,6},{8,11},{9,8},{10,9... | collective-permute-start | bytes 1572872 | tf_op jit(solution)/shard_map/ppermute | solution.py:67
  319.7 54.0 %collective-permute-start.25 = (bf16[128,2048]{1,0:T(8,128)(2,1)}, bf16[128,2048]{1,0:T(8,128)(2,1)}, u32[]{:S(2)}, u32[]{:S(2)}) collective-permute-start(bf16[128,2048]{1,0:T(8,128)(2,1)} %get-tuple-element.266), channel_id=1, source_target_pairs={{0,3},{1,0},{2,1},{3,2},{4,7},{5,4},{6,5},{7,6},{8,11},{9,8},{10,9... | collective-permute-start | bytes 1572872 | tf_op jit(solution)/shard_map/ppermute | solution.py:145
  321.8 51.9 %collective-permute-start.26 = (bf16[128,2048]{1,0:T(8,128)(2,1)}, bf16[128,2048]{1,0:T(8,128)(2,1)}, u32[]{:S(2)}, u32[]{:S(2)}) collective-permute-start(bf16[128,2048]{1,0:T(8,128)(2,1)} %get-tuple-element.265), channel_id=1, source_target_pairs={{0,1},{1,2},{2,3},{3,0},{4,5},{5,6},{6,7},{7,4},{8,9},{9,10},{10,1... | collective-permute-start | bytes 1572872 | tf_op jit(solution)/shard_map/ppermute | solution.py:145
  373.7 26.1 %all-to-all-start.3 = ((bf16[8,784,128]{2,1,0:T(8,128)(2,1)}), bf16[8,784,128]{2,1,0:T(8,128)(2,1)}, u32[]{:S(2)}, u32[]{:S(2)}) async-start(bf16[8,784,128]{2,1,0:T(8,128)(2,1)} %attend_back.1), calls=%async_computation.3 | async-start | bytes 3211264 | tf_op jit(solution)/shard_map/all_to_all | solution.py:1048
  378.2 107.7 %reduce-scatter.5.cloned.1.call-start = ((), (), s32[]{:S(2)}) async-start(), calls=%async_computation.12 | async-start | bytes 9437184 | tf_op jit(solution)/shard_map/reduce_scatter | solution.py:1137
  432.0 19.9 %collective-permute-start.30 = (bf16[128,2048]{1,0:T(8,128)(2,1)}, bf16[128,2048]{1,0:T(8,128)(2,1)S(1)}, u32[]{:S(2)}, u32[]{:S(2)}) collective-permute-start(bf16[128,2048]{1,0:T(8,128)(2,1)} %get-tuple-element.184), channel_id=1, source_target_pairs={{0,1},{1,2},{2,3},{3,0},{4,5},{5,6},{6,7},{7,4},{8,9},{9,10},{10,1... | collective-permute-start | bytes 1572872 | tf_op jit(solution)/shard_map/ppermute | solution.py:104
  451.9 23.1 %collective-permute-start.31 = (bf16[128,2048]{1,0:T(8,128)(2,1)}, bf16[128,2048]{1,0:T(8,128)(2,1)}, u32[]{:S(2)}, u32[]{:S(2)}) collective-permute-start(bf16[128,2048]{1,0:T(8,128)(2,1)} %get-tuple-element.188), channel_id=1, source_target_pairs={{0,2},{1,3},{2,0},{3,1},{4,6},{5,7},{6,4},{7,5},{8,10},{9,11},{10,... | collective-permute-start | bytes 1572872 | tf_op jit(solution)/shard_map/ppermute | solution.py:145
  (93 other events, 961.3 us)
Sparse Core Ops, SparseCore 0:
  10.5 48.5 all-gather.4
  61.0 36.9 all-gather.6
  99.9 92.5 all-gather.8
  194.8 46.6 all-gather.10
  268.7 114.8 reduce-scatter.2
  415.3 70.5 reduce-scatter.4
where the time goes:
time: 507 us; the launch traced here: 497 us
  waiting for transfers between devices  203 us (40%)
  Pallas kernels  109 us (21%)
  starting transfers between devices  74.9 us (15%)
  local copies, waits for them, and re-layouts  33.1 us (7%)
  other arithmetic  25 us (5%)
  matrix products  23.9 us (5%)
  between operations  15.7 us (3%)
  blocking collectives  13.2 us (3%)
    pallas_call x1, Pallas kernels, attend_back(): pl.pallas_call(functools.partial(attend_back_kernel, slots, bucket_count)...  35.3 us
    ppermute x5, waiting for transfers between devices, gather_far(): back_two = lax.ppermute(passed, 'head', [(1, 0), (3, 1), (0, 2), (2, 3)])  32.5 us
    ppermute x3, waiting for transfers between devices, sum_near(): from_back = lax.ppermute(to_ahead, 'head', cyclic(4, 1))  31.2 us
    ppermute x5, waiting for transfers between devices, gather_small(): other = lax.ppermute(held, axis, [(i, i ^ bit) for i in range(count)])  30.5 us
    dot_general x4, matrix products, dot_nt(): lax.dot_general(left, right, (((1,), (1,)), ((), ())), preferred_element_...  23.9 us
    pallas_call x1, Pallas kernels, attend(): pl.pallas_call(functools.partial(attend_kernel, slots), in_specs=[smem_sp...  22 us
    unnamed x153, local copies, waits for them, and re-layouts  20.8 us
    ppermute x3, waiting for transfers between devices, sum_far(): return [lax.ppermute(parts[2], 'head', [(0, 1), (1, 3), (2, 0), (3, 2)])]  20.2 us
  transfers between devices with their start and end apart: 45, of which 26 were waited for; matrix products, arithmetic and copies ran while one was open for 12% of the time, Pallas kernels for 22%

commit v1 on v0

--- a/solution.py
+++ b/solution.py
@@ -2,7 +2,6 @@
 
 import jax
 import jax.numpy as jnp
-import numpy as np
 from jax import lax
 from jax.experimental import pallas as pl
 from jax.experimental.pallas import tpu as pltpu
@@ -847,10 +846,9 @@
     )(spot, mine, rest)
 
 
-def project_back_kernel(slots, packed_ref, weight_ref, scale_ref, mix_ref, left_ref, *refs):
-    x_refs, attn_refs = refs[:slots], refs[slots : 2 * slots]
-    product_ref, gain_ref = refs[2 * slots : 2 * slots + 2]
-    part_refs, grads_ref = refs[2 * slots + 2 : -1], refs[-1]
+def weigh_kernel(slots, packed_ref, mix_ref, left_ref, *refs):
+    attn_refs = refs[:slots]
+    product_ref, grads_ref = refs[slots:]
     heads = packed_ref.shape[0]
     rows = slots * SPAN
     half = rows // 2
@@ -868,6 +866,46 @@
             grads_ref[:, width + start : width + start + LANES] = key.astype(bf16)
             grads_ref[:, 2 * width + start : 2 * width + start + LANES] = value.astype(bf16)
 
+    product_ref[:, : 3 * width] = dot_tn(left_ref[...], grads_ref[...]).astype(bf16)
+    attn = jnp.concatenate([ref[...] for ref in attn_refs], axis=0)
+    product_ref[:, 3 * width :] = dot_tn(attn, mix_ref[...]).astype(bf16)
+
+
+def weigh(packed, mix, left, attn_slots):
+    slots = len(attn_slots)
+    heads = packed.shape[0]
+    rows, depth = left.shape
+    width = 3 * heads * HD
+    total = width + mix.shape[1]
+    tile = 512
+    return pl.pallas_call(
+        functools.partial(weigh_kernel, slots),
+        grid=(depth // tile,),
+        in_specs=[
+            pl.BlockSpec(packed.shape, lambda j: (0, 0, 0)),
+            pl.BlockSpec(mix.shape, lambda j: (0, 0)),
+            pl.BlockSpec((rows, tile), lambda j: (0, j)),
+        ]
+        + [pl.BlockSpec((SPAN, tile), lambda j: (0, j))] * slots,
+        out_specs=[
+            pl.BlockSpec((tile, total), lambda j: (j, 0)),
+            pl.BlockSpec((rows, width), lambda j: (0, 0)),
+        ],
+        out_shape=[
+            jax.ShapeDtypeStruct((depth, total), bf16),
+            jax.ShapeDtypeStruct((rows, width), bf16),
+        ],
+        compiler_params=pltpu.CompilerParams(vmem_limit_bytes=LARGE),
+        cost_estimate=pl.CostEstimate(
+            flops=2 * rows * depth * total, bytes_accessed=4 * depth * total, transcendentals=0
+        ),
+        name="weigh",
+    )(packed, mix, left, *attn_slots)
+
+
+def project_back_kernel(slots, grads_ref, weight_ref, scale_ref, *refs):
+    x_refs = refs[:slots]
+    gain_ref, *part_refs = refs[slots:]
     part = dot_nt(grads_ref[...], weight_ref[...])
     gain = jnp.zeros((1, part.shape[1]), f32)
     for s in range(slots):
@@ -876,47 +914,32 @@
         x_hat = x_refs[s][...].astype(f32) * scale_ref[span, :1]
         gain = gain + jnp.sum(part[span] * x_hat, axis=0, keepdims=True)
     gain_ref[...] = gain
-    product_ref[:, : 3 * width] = dot_tn(left_ref[...], grads_ref[...]).astype(bf16)
-    attn = jnp.concatenate([ref[...] for ref in attn_refs], axis=0)
-    product_ref[:, 3 * width :] = dot_tn(attn, mix_ref[...]).astype(bf16)
-
-
-def project_back(packed, weights, scale, mix, left, x_slots, attn_slots):
+
+
+def project_back(grads, weights, scale, x_slots):
     slots = len(x_slots)
     depth, width = weights.shape
     rows = slots * SPAN
-    tile = 256
+    tile = 512
     spans = [pl.BlockSpec((SPAN, tile), lambda j: (0, j))] * slots
-    total = width + mix.shape[1]
     return pl.pallas_call(
         functools.partial(project_back_kernel, slots),
         grid=(depth // tile,),
         in_specs=[
-            pl.BlockSpec(packed.shape, lambda j: (0, 0, 0)),
+            pl.BlockSpec((rows, width), lambda j: (0, 0)),
             pl.BlockSpec((tile, width), lambda j: (j, 0)),
             pl.BlockSpec((rows, LANES), lambda j: (0, 0)),
-            pl.BlockSpec(mix.shape, lambda j: (0, 0)),
-            pl.BlockSpec((rows, tile), lambda j: (0, j)),
-        ]
-        + spans
-        + spans,
-        out_specs=[
-            pl.BlockSpec((tile, total), lambda j: (j, 0)),
-            pl.BlockSpec((1, tile), lambda j: (0, j)),
         ]
         + spans,
-        out_shape=[
-            jax.ShapeDtypeStruct((depth, total), bf16),
-            jax.ShapeDtypeStruct((1, depth), f32),
-        ]
+        out_specs=[pl.BlockSpec((1, tile), lambda j: (0, j))] + spans,
+        out_shape=[jax.ShapeDtypeStruct((1, depth), f32)]
         + [jax.ShapeDtypeStruct((SPAN, depth), bf16)] * slots,
-        scratch_shapes=[vmem((rows, width), bf16)],
         compiler_params=pltpu.CompilerParams(vmem_limit_bytes=LARGE),
         cost_estimate=pl.CostEstimate(
-            flops=4 * rows * depth * total, bytes_accessed=4 * depth * total, transcendentals=0
+            flops=2 * rows * depth * width, bytes_accessed=4 * depth * width, transcendentals=0
         ),
         name="project_back",
-    )(packed, weights, scale, mix, left, *x_slots, *attn_slots)
+    )(grads, weights, scale, *x_slots)
 
 
 def pair_kernel(slots, groups, *refs):
@@ -945,7 +968,7 @@
     slots, groups = len(left_one), len(right_one)
     rows, depth = slots * SPAN, left_one[0].shape[1]
     width = right_one[0].shape[1] + right_two[0].shape[1]
-    block = 256
+    block = 512
 
     def whole(array):
         return pl.BlockSpec(array.shape, lambda j: (0, 0))
@@ -1073,13 +1096,13 @@
     grad_near, out_slots = moved[: len(grad_near)], moved[len(grad_near) :]
     packed_mix, *grad_slots = together(to_rows(mixed), *gather_far(grad_near))
     attn_mix, *out_parts = out_project(packed_mix, full_out, slots)
-    out_parts, out_slots = together(out_parts, out_slots)
-    full_rest = lax.all_gather(jnp.concatenate(out_slots[1:]), "blk", axis=1, tiled=True)
     tokens_wide = tokens.astype(f32)
     hidden_one = tokens_wide + sum_terms(sum_near(out_parts, sum_far(out_parts))[0])
     rstd_two = rms_scale(hidden_one)
     normed_two = (hidden_one * rstd_two * gain_two).astype(bf16)
 
+    normed_two, out_slots = together(normed_two, out_slots)
+    full_rest = lax.all_gather(jnp.concatenate(out_slots[1:]), "blk", axis=1, tiled=True)
     normed_slots = gather_far(gather_near(normed_two))
     active, d_both = feed(normed_slots, grad_slots, full_ffn)
 
@@ -1115,7 +1138,7 @@
         block_order, ends, info, swapped, to_all(mix_grads), exact, lse, bias_rows, bucket_rows,
         slots, bucket_count,
     )
-    grads, *moved = together(grads, *moved)
+    grads, down_parts, *moved = together(grads, down_parts, *moved)
     attn_near, down_terms = moved[: 2 - slots], moved[2 - slots :]
     grads, *attn_slots = together(swap(grads), *gather_far(attn_near))
     extra = grads[:, -EXTRA:, 0].astype(f32).reshape(blk_count, 2, -1).sum(axis=1)
@@ -1123,16 +1146,15 @@
     if shares > 1:
         grads = grads.reshape((heads, shares) + grads.shape[1:])
         grads = jnp.sum(grads.astype(f32), axis=1).astype(bf16)
-    grad_heads, gain_part_one, *one_parts = project_back(
-        grads, full_qkv, scale_one, attn_mix, normed_one, token_slots, attn_slots
-    )
+    grad_heads, d_qkv = weigh(grads, attn_mix, normed_one, attn_slots)
+    grad_heads, grad_hidden = together(grad_heads, grad_hidden)
+    gain_part_one, *one_parts = project_back(d_qkv, full_qkv, scale_one, token_slots)
 
     one_far = sum_far(one_parts)
     gain_parts = jnp.stack(
         [part.reshape(blk_count, slots, gain_size) for part in (gain_part_one, gain_part_two)],
         axis=2,
     )
-    grad_heads, grad_hidden = together(grad_heads, grad_hidden)
     gain_parts, *one_far = together(gain_parts, *one_far)
     grad_heads = lax.psum_scatter(grad_heads, "blk", scatter_dimension=0, tiled=True).astype(f32)
     one_near, unused = sum_near(one_parts, one_far)
@@ -1140,9 +1162,10 @@
     gain_sums, down_parts, grad_hidden, *one_near = together(
         gain_sums, down_parts, grad_hidden, *one_near
     )
+    far_term = sum_direct(down_parts, [middle])
     gain_sums = scatter_head(gain_sums)
     grad_hidden = grad_hidden.astype(f32)
-    output = hidden_one + sum_all([down_parts[0]] + down_terms + sum_direct(down_parts, [middle]))
+    output = hidden_one + sum_all([down_parts[0]] + down_terms + far_term)
     d_normed_one = sum_terms(one_near)
     d_source_one, unused = norm_back(d_normed_one, tokens_wide, rms_scale(tokens_wide), gain_one)
     input_grad = d_hidden_one + d_source_one

time: 507 us -> 504 us (level)
  the two profiles are of different devices: /device:TPU:0 before, /device:TPU:2 now
where the time goes in v1:
time: 504 us; the launch traced here: 495 us
  waiting for transfers between devices  203 us (40%)
  Pallas kernels  110 us (22%)
  starting transfers between devices  72.2 us (14%)
  local copies, waits for them, and re-layouts  29.6 us (6%)
  other arithmetic  27.9 us (6%)
  matrix products  22.9 us (5%)
  between operations  15.6 us (3%)
  blocking collectives  13.6 us (3%)
    pallas_call x1, Pallas kernels, attend_back(): pl.pallas_call(functools.partial(attend_back_kernel, slots, bucket_count)...  35.3 us
    ppermute x5, waiting for transfers between devices, gather_small(): other = lax.ppermute(held, axis, [(i, i ^ bit) for i in range(count)])  31.3 us
    ppermute x5, waiting for transfers between devices, gather_far(): back_two = lax.ppermute(passed, 'head', [(1, 0), (3, 1), (0, 2), (2, 3)])  30 us
    ppermute x3, waiting for transfers between devices, sum_near(): from_ahead = lax.ppermute(to_back, 'head', cyclic(4, 3))  25.5 us
    ppermute x3, waiting for transfers between devices, sum_far(): return [lax.ppermute(parts[2], 'head', [(0, 1), (1, 3), (2, 0), (3, 2)])]  23.9 us
    dot_general x4, matrix products, dot_nt(): lax.dot_general(left, right, (((1,), (1,)), ((), ())), preferred_element_...  22.9 us
    ppermute x3, waiting for transfers between devices, sum_near(): from_back = lax.ppermute(to_ahead, 'head', cyclic(4, 1))  22.6 us
    pallas_call x1, Pallas kernels, attend(): pl.pallas_call(functools.partial(attend_kernel, slots), in_specs=[smem_sp...  22 us
  transfers between devices with their start and end apart: 45, of which 24 were waited for; matrix products, arithmetic and copies ran while one was open for 13% of the time, Pallas kernels for 22%

profile of v1, /device:TPU:2, one launch (start us, length us, event | category | flops | bytes accessed | tf_op | source)
XLA Modules:
  0.0 494.6 jit_solution(4719527334431036543)
XLA Ops:
  16.1 22.2 %collective-permute-done.3 = f32[1,1,160]{2,0,1:T(1,128)S(1)} collective-permute-done((f32[1,1,160]{2,0,1:T(1,128)S(1)}, f32[1,1,160]{2,0,1:T(1,128)S(1)}, u32[]{:S(2)}, u32[]{:S(2)}) %collective-permute-start.3) | collective-permute-done | bytes 672 | tf_op jit(solution)/shard_map/ppermute | solution.py:132
  87.0 5.7 %collective-permute-done.9 = bf16[512,256]{1,0:T(8,128)(2,1)S(1)} collective-permute-done((bf16[512,256]{1,0:T(8,128)(2,1)S(1)}, bf16[512,256]{1,0:T(8,128)(2,1)S(1)}, u32[]{:S(2)}, u32[]{:S(2)}) %collective-permute-start.9) | collective-permute-done | bytes 262176 | tf_op jit(solution)/shard_map/ppermute | solution.py:66
  92.7 6.2 %all-to-all-done.x_ref = bf16[8,768,128]{2,1,0:T(8,128)(2,1)} async-done(((bf16[8,768,128]{2,1,0:T(8,128)(2,1)}), bf16[8,768,128]{2,1,0:T(8,128)(2,1)}, u32[]{:S(2)}, u32[]{:S(2)}) %all-to-all-start) | async-done | bytes 1572896 | tf_op jit(solution)/shard_map/all_to_all | solution.py:1071
  101.4 22.0 %attend.1 = (bf16[8,256,128]{2,1,0:T(8,128)(2,1)S(1)}, f32[64,4096]{1,0:T(8,128)S(1)}, f32[1,4096]{1,0:T(1,128)S(1)}) custom-call(s32[32]{0:T(128)S(1)} %copy-done.30, s32[2]{0:T(128)S(1)} %bitcast.44, s32[3]{0:T(128)S(1)} %pad_add_fusion.2.info_ref, bf16[8,768,128]{2,1,0:T(8,128)(2,1)} %all-to-all-done.x_ref, f32[8,256]{1,0:T(8,128)S(1)} %select_reduce_fusion.bias_ref), custom_call_target="tpu_custom_call" | custom-call | flops 2147483648 | bytes 8388608 | tf_op jit(solution)/shard_map/attend/pallas_call | solution.py:483
  125.2 13.6 %all_to_all.25.packed_ref = bf16[8,256,128]{2,1,0:T(8,128)(2,1)S(1)} all-to-all(bf16[8,256,128]{2,1,0:T(8,128)(2,1)S(1)} %get-tuple-element.119), channel_id=1, replica_groups=mesh['blk'=8,'head'=4] {'blk'}, dimensions={0} | all-to-all | bytes 1048576 | tf_op jit(solution)/shard_map/all_to_all | solution.py:1071
  144.5 13.3 %collective-permute-done.14 = bf16[128,2048]{1,0:T(8,128)(2,1)S(1)} collective-permute-done((bf16[128,2048]{1,0:T(8,128)(2,1)S(1)}, bf16[128,2048]{1,0:T(8,128)(2,1)S(1)}, u32[]{:S(2)}, u32[]{:S(2)}) %collective-permute-start.14) | collective-permute-done | bytes 524320 | tf_op jit(solution)/shard_map/ppermute | solution.py:88
  162.0 12.8 %collective-permute-done.16 = bf16[128,2048]{1,0:T(8,128)(2,1)S(1)} collective-permute-done((bf16[128,2048]{1,0:T(8,128)(2,1)S(1)}, bf16[128,2048]{1,0:T(8,128)(2,1)S(1)}, u32[]{:S(2)}, u32[]{:S(2)}) %collective-permute-start.16) | collective-permute-done | bytes 524320 | tf_op jit(solution)/shard_map/ppermute | solution.py:103
  174.8 8.3 %collective-permute-done.15 = bf16[128,2048]{1,0:T(8,128)(2,1)} collective-permute-done((bf16[128,2048]{1,0:T(8,128)(2,1)S(1)}, bf16[128,2048]{1,0:T(8,128)(2,1)}, u32[]{:S(2)}, u32[]{:S(2)}) %collective-permute-start.15) | collective-permute-done | bytes 524320 | tf_op jit(solution)/shard_map/ppermute | solution.py:102
  190.2 12.8 %collective-permute-done.17.refs_1_ = bf16[128,2048]{1,0:T(8,128)(2,1)S(1)} collective-permute-done((bf16[128,2048]{1,0:T(8,128)(2,1)S(1)}, bf16[128,2048]{1,0:T(8,128)(2,1)S(1)}, u32[]{:S(2)}, u32[]{:S(2)}) %collective-permute-start.17) | collective-permute-done | bytes 524320 | tf_op jit(solution)/shard_map/ppermute | solution.py:66
  203.1 7.7 %collective-permute-done.18.refs_3_ = bf16[128,2048]{1,0:T(8,128)(2,1)S(1)} collective-permute-done((bf16[128,2048]{1,0:T(8,128)(2,1)S(1)}, bf16[128,2048]{1,0:T(8,128)(2,1)S(1)}, u32[]{:S(2)}, u32[]{:S(2)}) %collective-permute-start.18) | collective-permute-done | bytes 524320 | tf_op jit(solution)/shard_map/ppermute | solution.py:66
  212.9 10.9 %collective-permute-done.19.refs_2_ = bf16[128,2048]{1,0:T(8,128)(2,1)S(1)} collective-permute-done((bf16[128,2048]{1,0:T(8,128)(2,1)S(1)}, bf16[128,2048]{1,0:T(8,128)(2,1)S(1)}, u32[]{:S(2)}, u32[]{:S(2)}) %collective-permute-start.19) | collective-permute-done | bytes 524320 | tf_op jit(solution)/shard_map/ppermute | solution.py:75
  224.6 14.7 %feed.1 = (bf16[512,1280]{1,0:T(8,128)(2,1)}, bf16[512,2560]{1,0:T(8,128)(2,1)}) custom-call(bf16[128,2048]{1,0:T(8,128)(2,1)} %copy-done.5, bf16[128,2048]{1,0:T(8,128)(2,1)} %copy-done.11, bf16[128,2048]{1,0:T(8,128)(2,1)} %copy-done.22, bf16[128,2048]{1,0:T(8,128)(2,1)} %copy-done.13, bf16[128,2048]{1,0:T(8,128)(2,1)} %refs_4_.1, ...), custom_call_target="tpu_custom_call" | custom-call | flops 8053063680 | bytes 15728640 | tf_op jit(solution)/shard_map/feed/pallas_call | solution.py:797
  239.4 9.3 %fusion.4 = bf16[512,2048]{1,0:T(8,128)(2,1)S(1)} fusion(bf16[512,2560]{1,0:T(8,128)(2,1)} %get-tuple-element.138.refs_8_, bf16[2048,3840]{1,0:T(8,128)(2,1)} %all-gather.9.cloned.1.call-done.refs_8_.refs_9_.refs_10_), kind=kOutput, calls=%fused_computation.4 | convolution fusion | flops 5369757696 | bytes 15204352 | tf_op jit(solution)/shard_map/dot_general | solution.py:47
  252.5 11.7 %pair_product.1 = bf16[2048,3840]{1,0:T(8,128)(2,1)} custom-call(bf16[128,2048]{1,0:T(8,128)(2,1)S(1)} %copy-done.6, bf16[128,2048]{1,0:T(8,128)(2,1)S(1)} %copy-done.12, bf16[128,2048]{1,0:T(8,128)(2,1)S(1)} %copy-done.23, bf16[128,2048]{1,0:T(8,128)(2,1)S(1)} %copy-done.14, bf16[128,2048]{1,0:T(8,128)(2,1)S(1)} %copy-done.4, ...), custom_call_target="tpu_custom_call" | custom-call | flops 8053063680 | bytes 15728640 | tf_op jit(solution)/shard_map/pair_product/pallas_call | solution.py:976
  268.8 7.1 %fusion.7 = bf16[512,2048]{1,0:T(8,128)(2,1)} fusion(bf16[512,1280]{1,0:T(8,128)(2,1)S(1)} %copy-done.28, bf16[2048,3840]{1,0:T(8,128)(2,1)} %all-gather.9.cloned.1.call-done.refs_8_.refs_9_.refs_10_), kind=kOutput, calls=%fused_computation.5 | convolution fusion | flops 2685403136 | bytes 8650752 | tf_op jit(solution)/shard_map/dot_general | solution.py:47
  276.0 14.2 %collective-permute-done.21 = bf16[128,2048]{1,0:T(8,128)(2,1)S(1)} collective-permute-done((bf16[128,2048]{1,0:T(8,128)(2,1)}, bf16[128,2048]{1,0:T(8,128)(2,1)S(1)}, u32[]{:S(2)}, u32[]{:S(2)}) %collective-permute-start.21) | collective-permute-done | bytes 524320 | tf_op jit(solution)/shard_map/ppermute | solution.py:102
  314.7 16.2 %all-to-all-done.2.mixed_ref = bf16[32,64,128]{2,1,0:T(8,128)(2,1)S(1)} async-done(((bf16[32,64,128]{2,1,0:T(8,128)(2,1)}), bf16[32,64,128]{2,1,0:T(8,128)(2,1)S(1)}, u32[]{:S(2)}, u32[]{:S(2)}) %all-to-all-start.2) | async-done | bytes 524320 | tf_op jit(solution)/shard_map/all_to_all | solution.py:1075
  330.9 35.3 %attend_back.1 = bf16[8,784,128]{2,1,0:T(8,128)(2,1)} custom-call(s32[32]{0:T(128)S(1)} %copy-done.30, s32[2]{0:T(128)S(1)} %bitcast.45, s32[3]{0:T(128)S(1)} %pad_add_fusion.2.info_ref, bf16[8,768,128]{2,1,0:T(8,128)(2,1)} %all-to-all-done.x_ref, bf16[32,64,128]{2,1,0:T(8,128)(2,1)S(1)} %all-to-all-done.2.mixed_ref, f32[64,4096]{1,0:T(8,128)S(1)} %copy-done.33, ...), custom_call_target="tpu_custom_call" | custom-call | flops 5368709120 | bytes 12582912 | tf_op jit(solution)/shard_map/attend_back/pallas_call | solution.py:686
  373.2 14.1 %collective-permute-done.27.refs_2_ = bf16[128,2048]{1,0:T(8,128)(2,1)S(1)} collective-permute-done((bf16[128,2048]{1,0:T(8,128)(2,1)S(1)}, bf16[128,2048]{1,0:T(8,128)(2,1)S(1)}, u32[]{:S(2)}, u32[]{:S(2)}) %collective-permute-start.27) | collective-permute-done | bytes 524320 | tf_op jit(solution)/shard_map/ppermute | solution.py:75
  392.1 10.0 %weigh.1 = (bf16[2048,2048]{1,0:T(8,128)(2,1)}, bf16[512,1536]{1,0:T(8,128)(2,1)}) custom-call(bf16[8,784,128]{2,1,0:T(8,128)(2,1)} %all-to-all-done.3.packed_ref, bf16[512,512]{1,0:T(8,128)(2,1)} %copy-done.31, bf16[512,2048]{1,0:T(8,128)(2,1)} %copy-done.26, bf16[128,2048]{1,0:T(8,128)(2,1)} %copy-done.39, ...), custom_call_target="tpu_custom_call" | custom-call | flops 4294967296 | bytes 16777216 | tf_op jit(solution)/shard_map/weigh/pallas_call | solution.py:881
  402.1 7.9 %project_back.1 = (f32[1,2048]{1,0:T(1,128)}, bf16[128,2048]{1,0:T(8,128)(2,1)}, bf16[128,2048]{1,0:T(8,128)(2,1)}, bf16[128,2048]{1,0:T(8,128)(2,1)}, bf16[128,2048]{1,0:T(8,128)(2,1)}) custom-call(bf16[512,1536]{1,0:T(8,128)(2,1)} %get-tuple-element.169.grads_ref, bf16[2048,1536]{1,0:T(8,128)(2,1)} %all-gather.5.cloned.1.call-done.refs_5_.refs_6_.refs_7_.weight_ref, ...), custom_call_target="tpu_custom_call" | custom-call | flops 3221225472 | bytes 12582912 | tf_op jit(solution)/shard_map/project_back/pallas_call | solution.py:925
  414.2 10.7 %collective-permute-done.28 = bf16[128,2048]{1,0:T(8,128)(2,1)S(1)} collective-permute-done((bf16[128,2048]{1,0:T(8,128)(2,1)}, bf16[128,2048]{1,0:T(8,128)(2,1)S(1)}, u32[]{:S(2)}, u32[]{:S(2)}) %collective-permute-start.28) | collective-permute-done | bytes 524320 | tf_op jit(solution)/shard_map/ppermute | solution.py:88
  443.6 9.8 %collective-permute-done.30 = bf16[128,2048]{1,0:T(8,128)(2,1)S(1)} collective-permute-done((bf16[128,2048]{1,0:T(8,128)(2,1)}, bf16[128,2048]{1,0:T(8,128)(2,1)S(1)}, u32[]{:S(2)}, u32[]{:S(2)}) %collective-permute-start.30) | collective-permute-done | bytes 524320 | tf_op jit(solution)/shard_map/ppermute | solution.py:103
  467.4 10.8 %collective-permute-done.33 = f32[2,64]{1,0:T(2,128)S(1)} collective-permute-done((f32[2,64]{1,0:T(2,128)S(1)}, f32[2,64]{1,0:T(2,128)S(1)}, u32[]{:S(2)}, u32[]{:S(2)}) %collective-permute-start.33) | collective-permute-done | bytes 544 | tf_op jit(solution)/shard_map/ppermute | solution.py:163
  (294 shorter events, 171.6 us)
Async XLA Ops:
  7.2 50.4 %all-gather.5.cloned.1.call-start = ((), (), s32[]{:S(2)}) async-start(), calls=%async_computation.7 | async-start | bytes 7077888 | tf_op jit(solution)/shard_map/all_gather | solution.py:1041
  9.4 129.4 %all-gather.7.cloned.1.call-start = ((), (), s32[]{:S(2)}) async-start(), calls=%async_computation.8 | async-start | bytes 2359296 | tf_op jit(solution)/shard_map/all_gather | solution.py:1044
  10.2 213.6 %all-gather.9.cloned.1.call-start = ((), (), s32[]{:S(2)}) async-start(), calls=%async_computation.9 | async-start | bytes 17694720 | tf_op jit(solution)/shard_map/all_gather | solution.py:1045
  12.0 31.0 %collective-permute-start = (bf16[128,2048]{1,0:T(8,128)(2,1)S(1)}, bf16[128,2048]{1,0:T(8,128)(2,1)S(1)}, u32[]{:S(2)}, u32[]{:S(2)}) collective-permute-start(bf16[128,2048]{1,0:T(8,128)(2,1)S(1)} %copy-done.1), channel_id=1, source_target_pairs={{0,1},{1,2},{2,3},{3,0},{4,5},{5,6},{6,7},{7,4},{8,9},{9,10},{10,1... | collective-permute-start | bytes 1572872 | tf_op jit(solution)/shard_map/ppermute | solution.py:66
  13.7 29.4 %collective-permute-start.1 = (bf16[128,2048]{1,0:T(8,128)(2,1)S(1)}, bf16[128,2048]{1,0:T(8,128)(2,1)S(1)}, u32[]{:S(2)}, u32[]{:S(2)}) collective-permute-start(bf16[128,2048]{1,0:T(8,128)(2,1)S(1)} %copy-done.1), channel_id=1, source_target_pairs={{0,3},{1,0},{2,1},{3,2},{4,7},{5,4},{6,5},{7,6},{8,11},{9,8},{10,9... | collective-permute-start | bytes 1572872 | tf_op jit(solution)/shard_map/ppermute | solution.py:66
  68.8 30.1 %all-to-all-start = ((bf16[8,768,128]{2,1,0:T(8,128)(2,1)}), bf16[8,768,128]{2,1,0:T(8,128)(2,1)}, u32[]{:S(2)}, u32[]{:S(2)}) async-start(bf16[8,768,128]{2,1,0:T(8,128)(2,1)} %copy-done.19), calls=%async_computation | async-start | bytes 3145728 | tf_op jit(solution)/shard_map/all_to_all | solution.py:1071
  73.6 202.3 %all-gather.11.cloned.1.call-start = ((), (), s32[]{:S(2)}) async-start(), calls=%async_computation.10 | async-start | bytes 7077888 | tf_op jit(solution)/shard_map/all_gather | solution.py:1105
  81.7 41.7 %collective-permute-start.10 = (bf16[128,2048]{1,0:T(8,128)(2,1)S(1)}, bf16[128,2048]{1,0:T(8,128)(2,1)S(1)}, u32[]{:S(2)}, u32[]{:S(2)}) collective-permute-start(bf16[128,2048]{1,0:T(8,128)(2,1)S(1)} %copy-done.3), channel_id=1, source_target_pairs={{0,1},{1,2},{2,3},{3,0},{4,5},{5,6},{6,7},{7,4},{8,9},{9,10},{10,1... | collective-permute-start | bytes 1572872 | tf_op jit(solution)/shard_map/ppermute | solution.py:66
  81.8 41.7 %collective-permute-start.11 = (bf16[128,2048]{1,0:T(8,128)(2,1)S(1)}, bf16[128,2048]{1,0:T(8,128)(2,1)S(1)}, u32[]{:S(2)}, u32[]{:S(2)}) collective-permute-start(bf16[128,2048]{1,0:T(8,128)(2,1)S(1)} %copy-done.3), channel_id=1, source_target_pairs={{0,3},{1,0},{2,1},{3,2},{4,7},{5,4},{6,5},{7,6},{8,11},{9,8},{10,9... | collective-permute-start | bytes 1572872 | tf_op jit(solution)/shard_map/ppermute | solution.py:66
  98.9 24.6 %collective-permute-start.12 = (bf16[512,256]{1,0:T(8,128)(2,1)S(1)}, bf16[512,256]{1,0:T(8,128)(2,1)S(1)}, u32[]{:S(2)}, u32[]{:S(2)}) collective-permute-start(bf16[512,256]{1,0:T(8,128)(2,1)S(1)} %select_select_fusion.4), channel_id=1, source_target_pairs={{1,0},{3,1},{0,2},{2,3},{5,4},{7,5},{4,6},{6,7},{9,8},{11,9},{8,10... | collective-permute-start | bytes 786440 | tf_op jit(solution)/shard_map/ppermute | solution.py:75
  158.8 24.3 %collective-permute-start.15 = (bf16[128,2048]{1,0:T(8,128)(2,1)S(1)}, bf16[128,2048]{1,0:T(8,128)(2,1)}, u32[]{:S(2)}, u32[]{:S(2)}) collective-permute-start(bf16[128,2048]{1,0:T(8,128)(2,1)S(1)} %get-tuple-element.128), channel_id=1, source_target_pairs={{0,3},{1,0},{2,1},{3,2},{4,7},{5,4},{6,5},{7,6},{8,11},{9,8},{10,9... | collective-permute-start | bytes 1572872 | tf_op jit(solution)/shard_map/ppermute | solution.py:102
  186.3 215.8 %reduce-scatter.3.cloned.1.call-start = ((), (), s32[]{:S(2)}) async-start(), calls=%async_computation.11 | async-start | bytes 17694720 | tf_op jit(solution)/shard_map/reduce_scatter | solution.py:1117
  187.1 23.7 %collective-permute-start.18 = (bf16[128,2048]{1,0:T(8,128)(2,1)S(1)}, bf16[128,2048]{1,0:T(8,128)(2,1)S(1)}, u32[]{:S(2)}, u32[]{:S(2)}) collective-permute-start(bf16[128,2048]{1,0:T(8,128)(2,1)S(1)} %multiply_convert_fusion.refs_0_), channel_id=1, source_target_pairs={{0,3},{1,0},{2,1},{3,2},{4,7},{5,4},{6,5},{7,6},{8,11},{9,8},{10,9... | collective-permute-start | bytes 1572872 | tf_op jit(solution)/shard_map/ppermute | solution.py:66
  266.8 23.4 %collective-permute-start.21 = (bf16[128,2048]{1,0:T(8,128)(2,1)}, bf16[128,2048]{1,0:T(8,128)(2,1)S(1)}, u32[]{:S(2)}, u32[]{:S(2)}) collective-permute-start(bf16[128,2048]{1,0:T(8,128)(2,1)} %get-tuple-element.145), channel_id=1, source_target_pairs={{0,3},{1,0},{2,1},{3,2},{4,7},{5,4},{6,5},{7,6},{8,11},{9,8},{10,9... | collective-permute-start | bytes 1572872 | tf_op jit(solution)/shard_map/ppermute | solution.py:102
  267.9 22.3 %collective-permute-start.22 = (bf16[128,2048]{1,0:T(8,128)(2,1)}, bf16[128,2048]{1,0:T(8,128)(2,1)}, u32[]{:S(2)}, u32[]{:S(2)}) collective-permute-start(bf16[128,2048]{1,0:T(8,128)(2,1)} %get-tuple-element.146), channel_id=1, source_target_pairs={{0,1},{1,2},{2,3},{3,0},{4,5},{5,6},{6,7},{7,4},{8,9},{9,10},{10,1... | collective-permute-start | bytes 1572872 | tf_op jit(solution)/shard_map/ppermute | solution.py:103
  301.4 29.5 %all-to-all-start.2 = ((bf16[32,64,128]{2,1,0:T(8,128)(2,1)}), bf16[32,64,128]{2,1,0:T(8,128)(2,1)S(1)}, u32[]{:S(2)}, u32[]{:S(2)}) async-start(bf16[32,64,128]{2,1,0:T(8,128)(2,1)} %bitcast.14), calls=%async_computation.2 | async-start | bytes 1048576 | tf_op jit(solution)/shard_map/all_to_all | solution.py:1075
  305.8 60.5 %collective-permute-start.23 = (bf16[128,2048]{1,0:T(8,128)(2,1)}, bf16[128,2048]{1,0:T(8,128)(2,1)}, u32[]{:S(2)}, u32[]{:S(2)}) collective-permute-start(bf16[128,2048]{1,0:T(8,128)(2,1)} %copy-done.39), channel_id=1, source_target_pairs={{0,1},{1,2},{2,3},{3,0},{4,5},{5,6},{6,7},{7,4},{8,9},{9,10},{10,1... | collective-permute-start | bytes 1572872 | tf_op jit(solution)/shard_map/ppermute | solution.py:66
  307.3 59.0 %collective-permute-start.24 = (bf16[128,2048]{1,0:T(8,128)(2,1)}, bf16[128,2048]{1,0:T(8,128)(2,1)}, u32[]{:S(2)}, u32[]{:S(2)}) collective-permute-start(bf16[128,2048]{1,0:T(8,128)(2,1)} %copy-done.39), channel_id=1, source_target_pairs={{0,3},{1,0},{2,1},{3,2},{4,7},{5,4},{6,5},{7,6},{8,11},{9,8},{10,9... | collective-permute-start | bytes 1572872 | tf_op jit(solution)/shard_map/ppermute | solution.py:66
  312.5 53.7 %collective-permute-start.25 = (bf16[128,2048]{1,0:T(8,128)(2,1)}, bf16[128,2048]{1,0:T(8,128)(2,1)}, u32[]{:S(2)}, u32[]{:S(2)}) collective-permute-start(bf16[128,2048]{1,0:T(8,128)(2,1)} %get-tuple-element.265), channel_id=1, source_target_pairs={{0,3},{1,0},{2,1},{3,2},{4,7},{5,4},{6,5},{7,6},{8,11},{9,8},{10,9... | collective-permute-start | bytes 1572872 | tf_op jit(solution)/shard_map/ppermute | solution.py:144
  314.3 51.9 %collective-permute-start.26 = (bf16[128,2048]{1,0:T(8,128)(2,1)}, bf16[128,2048]{1,0:T(8,128)(2,1)}, u32[]{:S(2)}, u32[]{:S(2)}) collective-permute-start(bf16[128,2048]{1,0:T(8,128)(2,1)} %get-tuple-element.263), channel_id=1, source_target_pairs={{0,1},{1,2},{2,3},{3,0},{4,5},{5,6},{6,7},{7,4},{8,9},{9,10},{10,1... | collective-permute-start | bytes 1572872 | tf_op jit(solution)/shard_map/ppermute | solution.py:144
  366.3 25.8 %all-to-all-start.3 = ((bf16[8,784,128]{2,1,0:T(8,128)(2,1)}), bf16[8,784,128]{2,1,0:T(8,128)(2,1)}, u32[]{:S(2)}, u32[]{:S(2)}) async-start(bf16[8,784,128]{2,1,0:T(8,128)(2,1)} %attend_back.1), calls=%async_computation.3 | async-start | bytes 3211264 | tf_op jit(solution)/shard_map/all_to_all | solution.py:1071
  371.2 112.3 %reduce-scatter.5.cloned.1.call-start = ((), (), s32[]{:S(2)}) async-start(), calls=%async_computation.12 | async-start | bytes 9437184 | tf_op jit(solution)/shard_map/reduce_scatter | solution.py:1159
  430.9 22.5 %collective-permute-start.30 = (bf16[128,2048]{1,0:T(8,128)(2,1)}, bf16[128,2048]{1,0:T(8,128)(2,1)S(1)}, u32[]{:S(2)}, u32[]{:S(2)}) collective-permute-start(bf16[128,2048]{1,0:T(8,128)(2,1)} %get-tuple-element.184), channel_id=1, source_target_pairs={{0,1},{1,2},{2,3},{3,0},{4,5},{5,6},{6,7},{7,4},{8,9},{9,10},{10,1... | collective-permute-start | bytes 1572872 | tf_op jit(solution)/shard_map/ppermute | solution.py:103
  453.4 25.2 %collective-permute-start.31 = (bf16[128,2048]{1,0:T(8,128)(2,1)}, bf16[128,2048]{1,0:T(8,128)(2,1)}, u32[]{:S(2)}, u32[]{:S(2)}) collective-permute-start(bf16[128,2048]{1,0:T(8,128)(2,1)} %get-tuple-element.188), channel_id=1, source_target_pairs={{0,2},{1,3},{2,0},{3,1},{4,6},{5,7},{6,4},{7,5},{8,10},{9,11},{10,... | collective-permute-start | bytes 1572872 | tf_op jit(solution)/shard_map/ppermute | solution.py:144
  (84 other events, 915.3 us)
Sparse Core Ops, SparseCore 0:
  10.5 47.0 all-gather.4
  59.5 38.4 all-gather.6
  100.0 91.0 all-gather.8
  193.4 46.6 all-gather.10
  264.3 117.7 reduce-scatter.2
  402.2 71.4 reduce-scatter.4
